TPU v7x, 32 devices: a whole 2x2x4 slice. The times are simulated.
32 devices in a mesh: seq: 4 (over x, core), dp: 8 (over z, y).
Axes of the slice: x: 2, y: 2, z: 4, core: 2. Of those that a mesh axis runs over, the one named last changes fastest.
Arguments:
- tokens: bfloat16 [8, 512, 768], P('dp', 'seq'), may hold values from -6 to 6
- memory: bfloat16 [8, 1024, 768], P('dp', 'seq'), may hold values from -6 to 6
- target_segments: int32 [8, 512], P('dp'), may hold values from 0 to 254, as said below
- memory_segments: int32 [8, 1024], P('dp'), may hold values from 0 to 254, as said below
- pad_counts: int32 [8, 2], P('dp'), may hold values from 0 to 252, as said below
- out_grad: bfloat16 [8, 512, 768], P('dp', 'seq'), may hold values from -6 to 6
- self_query: bfloat16 [768, 768], replicated, may hold values from -0.21875 to 0.21875
- self_key: bfloat16 [768, 768], replicated, may hold values from -0.21875 to 0.21875
- self_value: bfloat16 [768, 768], replicated, may hold values from -0.21875 to 0.21875
- self_out: bfloat16 [768, 768], replicated, may hold values from -0.875 to 0.875
- cross_query: bfloat16 [768, 768], replicated, may hold values from -0.21875 to 0.21875
- cross_key: bfloat16 [768, 768], replicated, may hold values from -0.21875 to 0.21875
- cross_value: bfloat16 [768, 768], replicated, may hold values from -0.21875 to 0.21875
- cross_out: bfloat16 [768, 768], replicated, may hold values from -0.875 to 0.875
- feed_in: bfloat16 [768, 3072], replicated, may hold values from -0.21875 to 0.21875
- feed_out: bfloat16 [3072, 768], replicated, may hold values from -0.109375 to 0.109375
- gain_attend: bfloat16 [768], replicated, may hold values from 0.099609375 to 1.8984375
- shift_attend: bfloat16 [768], replicated, may hold values from -3 to 3
- gain_cross: bfloat16 [768], replicated, may hold values from 0.099609375 to 1.8984375
- shift_cross: bfloat16 [768], replicated, may hold values from -3 to 3
- gain_feed: bfloat16 [768], replicated, may hold values from 0.099609375 to 1.8984375
- shift_feed: bfloat16 [768], replicated, may hold values from -3 to 3
Outputs:
- layer_out: float32 [8, 512, 768], P('dp', 'seq')
- tokens_grad: float32 [8, 512, 768], P('dp', 'seq')
- memory_grad: float32 [8, 1024, 768], P('dp', 'seq')
- grad_self_query: float32 [768, 768], P('dp')
- grad_self_key: float32 [768, 768], P('dp')
- grad_self_value: float32 [768, 768], P('dp')
- grad_self_out: float32 [768, 768], P('dp')
- grad_cross_query: float32 [768, 768], P('dp')
- grad_cross_key: float32 [768, 768], P('dp')
- grad_cross_value: float32 [768, 768], P('dp')
- grad_cross_out: float32 [768, 768], P('dp')
- grad_feed_in: float32 [768, 3072], P('dp')
- grad_feed_out: float32 [3072, 768], P('dp')
- grad_gain_attend: float32 [768], P('dp')
- grad_shift_attend: float32 [768], P('dp')
- grad_gain_cross: float32 [768], P('dp')
- grad_shift_cross: float32 [768], P('dp')
- grad_gain_feed: float32 [768], P('dp')
- grad_shift_feed: float32 [768], P('dp')
Inputs may be any that keep to these rules, and one draw needn't show every extreme that they name: `target_segments`: in each row ids start at 0, never fall, and rise by at most one from one position to the next; the padded tail of a row continues its last document. `memory_segments`: in each row ids start at 0, never fall and rise by at most one from one position to the next; the unpadded memory of a row holds each id of the row's targets, every one of them, and no other. `pad_counts`: column 0 counts padded target positions, column 1 padded memory positions; the memory of a row's last document is never wholly padded; some row has no padding.
All inputs are finite; a program needn't handle non-finite values.
Results may differ from a plain program's by a relative error of at most 0.018.
Values may be sent and summed in bfloat16 or wider, within the bound.
A program may use at most 192 MiB of HBM per device.

v0:
```python
import jax
import jax.numpy as jnp
from jax import lax
from jax.sharding import PartitionSpec as P

HEAD_DIM = 64


EPSILON = 1e-05
NEGATIVE = -1e30


def layer_norm(values, gain_vec, shift_vec):
    row_mean = jnp.mean(values, axis=-1, keepdims=True)
    centered = values - row_mean
    spread = jnp.mean(centered * centered, axis=-1, keepdims=True)
    return centered * lax.rsqrt(spread + EPSILON) * gain_vec + shift_vec


def gelu_exact(values):
    return jax.nn.gelu(values, approximate=False)


def project(left_side, right_side):
    return jnp.dot(left_side, right_side, preferred_element_type=jnp.float32)


def project_back(left_side, right_side):
    return jnp.einsum("nd,ed->ne", left_side, right_side, preferred_element_type=jnp.float32)


def weight_grad(inputs, gradients):
    return jnp.einsum("nd,ne->de", inputs, gradients, preferred_element_type=jnp.float32)


def split_heads(values, row_count):
    return values.reshape(row_count, -1, values.shape[-1] // HEAD_DIM, HEAD_DIM)


def scores_of(head_query, head_key, allowed):
    scores = jnp.einsum(
        "rqhd,rkhd->rhqk", head_query, head_key, preferred_element_type=jnp.float32
    ) * HEAD_DIM ** (-0.5)
    return jnp.where(allowed[:, None], scores, NEGATIVE)


def attend(queries, keys_in, values_in, allowed, row_count):
    scores = scores_of(split_heads(queries, row_count), split_heads(keys_in, row_count), allowed)
    highest = jnp.max(scores, axis=-1, keepdims=True)
    exponent = jnp.exp(scores - highest)
    totals = jnp.sum(exponent, axis=-1, keepdims=True)
    weights = (exponent / totals).astype(jnp.bfloat16)
    mixture = jnp.einsum(
        "rhqk,rkhd->rqhd",
        weights,
        split_heads(values_in, row_count),
        preferred_element_type=jnp.float32,
    )
    return (mixture.reshape(queries.shape).astype(jnp.bfloat16), highest + jnp.log(totals))


def attend_back(queries, keys_in, values_in, allowed, log_total, grad_mixture, row_count):
    head_query = split_heads(queries, row_count)
    head_key = split_heads(keys_in, row_count)
    head_grad = split_heads(grad_mixture, row_count)
    weights = jnp.exp(scores_of(head_query, head_key, allowed) - log_total)
    grad_weights = jnp.einsum(
        "rqhd,rkhd->rhqk",
        head_grad,
        split_heads(values_in, row_count),
        preferred_element_type=jnp.float32,
    )
    grad_scores = (
        weights * (grad_weights - jnp.sum(weights * grad_weights, axis=-1, keepdims=True))
    ).astype(jnp.bfloat16)
    factor = HEAD_DIM ** (-0.5)
    grad_query = (
        jnp.einsum("rhqk,rkhd->rqhd", grad_scores, head_key, preferred_element_type=jnp.float32)
        * factor
    )
    grad_key = (
        jnp.einsum("rhqk,rqhd->rkhd", grad_scores, head_query, preferred_element_type=jnp.float32)
        * factor
    )
    grad_value = jnp.einsum(
        "rhqk,rqhd->rkhd",
        weights.astype(jnp.bfloat16),
        head_grad,
        preferred_element_type=jnp.float32,
    )
    return (
        grad_query.reshape(queries.shape),
        grad_key.reshape(keys_in.shape),
        grad_value.reshape(values_in.shape),
    )


def shards(
    tokens,
    memory,
    target_segments,
    memory_segments,
    pad_counts,
    out_grad,
    self_query,
    self_key,
    self_value,
    self_out,
    cross_query,
    cross_key,
    cross_value,
    cross_out,
    feed_in,
    feed_out,
    gain_attend,
    shift_attend,
    gain_cross,
    shift_cross,
    gain_feed,
    shift_feed,
):
    row_count, shard_len, width = tokens.shape
    seq_pieces = lax.axis_size("seq")
    seq_index = lax.axis_index("seq")
    full_len = shard_len * seq_pieces
    src_shard = memory.shape[1]
    src_full = src_shard * seq_pieces
    query_pos = seq_index * shard_len + jnp.arange(shard_len)
    key_pos = jnp.arange(full_len)
    own_segs = lax.dynamic_slice_in_dim(target_segments, seq_index * shard_len, shard_len, 1)
    target_valid = full_len - pad_counts[:, 0]
    memory_valid = src_full - pad_counts[:, 1]
    same_doc = target_segments[:, None, :] == own_segs[:, :, None]
    causal = key_pos[None, :] <= query_pos[:, None]
    key_alive = (key_pos[None, None, :] < target_valid[:, None, None]) | (
        key_pos[None, :] == query_pos[:, None]
    )[None]
    self_mask = same_doc & causal[None] & key_alive
    cross_mask = (memory_segments[:, None, :] == own_segs[:, :, None]) & (
        jnp.arange(src_full)[None, None, :] < memory_valid[:, None, None]
    )
    layer_in = tokens.reshape(row_count * shard_len, width).astype(jnp.float32)
    normed_attend, pull_attend = jax.vjp(
        layer_norm, layer_in, gain_attend.astype(jnp.float32), shift_attend.astype(jnp.float32)
    )
    hidden_attend = normed_attend.astype(jnp.bfloat16)
    query_rows = project(hidden_attend, self_query).astype(jnp.bfloat16)
    key_local = (
        project(hidden_attend, self_key).astype(jnp.bfloat16).reshape(row_count, shard_len, width)
    )
    value_local = (
        project(hidden_attend, self_value).astype(jnp.bfloat16).reshape(row_count, shard_len, width)
    )
    keys_all, values_all = (
        lax.all_gather(key_local, "seq", axis=1, tiled=True),
        lax.all_gather(value_local, "seq", axis=1, tiled=True),
    )
    self_mixed, self_total = attend(query_rows, keys_all, values_all, self_mask, row_count)
    after_self = layer_in + project(self_mixed, self_out)
    normed_cross, pull_cross = jax.vjp(
        layer_norm, after_self, gain_cross.astype(jnp.float32), shift_cross.astype(jnp.float32)
    )
    hidden_cross = normed_cross.astype(jnp.bfloat16)
    cross_rows = project(hidden_cross, cross_query).astype(jnp.bfloat16)
    memory_flat = memory.reshape(row_count * src_shard, width)
    memory_whole = lax.all_gather(memory, "seq", axis=1, tiled=True).reshape(
        row_count * src_full, width
    )
    memory_keys = (
        project(memory_whole, cross_key).astype(jnp.bfloat16).reshape(row_count, src_full, width)
    )
    memory_values = (
        project(memory_whole, cross_value).astype(jnp.bfloat16).reshape(row_count, src_full, width)
    )
    cross_mixed, cross_total = attend(cross_rows, memory_keys, memory_values, cross_mask, row_count)
    after_cross = after_self + project(cross_mixed, cross_out)
    normed_feed, pull_feed = jax.vjp(
        layer_norm, after_cross, gain_feed.astype(jnp.float32), shift_feed.astype(jnp.float32)
    )
    hidden_feed = normed_feed.astype(jnp.bfloat16)
    upward = project(hidden_feed, feed_in)
    activated, pull_gelu = jax.vjp(gelu_exact, upward)
    activated_low = activated.astype(jnp.bfloat16)
    layer_out = after_cross + project(activated_low, feed_out)
    grad_output = out_grad.reshape(row_count * shard_len, width)
    grad_feed_out = weight_grad(activated_low, grad_output)
    grad_upward = pull_gelu(project_back(grad_output, feed_out))[0].astype(jnp.bfloat16)
    grad_feed_in = weight_grad(hidden_feed, grad_upward)
    grad_in_feed, grad_gain_feed, grad_shift_feed = pull_feed(project_back(grad_upward, feed_in))
    grad_after_cross = grad_output.astype(jnp.float32) + grad_in_feed
    grad_cross_low = grad_after_cross.astype(jnp.bfloat16)
    grad_cross_out = weight_grad(cross_mixed, grad_cross_low)
    grad_cross_mixed = project_back(grad_cross_low, cross_out).astype(jnp.bfloat16)
    grad_cross_rows, memory_key_terms, memory_value_terms = attend_back(
        cross_rows, memory_keys, memory_values, cross_mask, cross_total, grad_cross_mixed, row_count
    )
    grad_memory_keys, grad_memory_values = (
        lax.psum_scatter(
            memory_key_terms.astype(jnp.bfloat16), "seq", scatter_dimension=1, tiled=True
        ).astype(jnp.float32),
        lax.psum_scatter(
            memory_value_terms.astype(jnp.bfloat16), "seq", scatter_dimension=1, tiled=True
        ).astype(jnp.float32),
    )
    grad_memory_keys = grad_memory_keys.reshape(row_count * src_shard, width).astype(jnp.bfloat16)
    grad_memory_values = grad_memory_values.reshape(row_count * src_shard, width).astype(
        jnp.bfloat16
    )
    grad_cross_key = weight_grad(memory_flat, grad_memory_keys)
    grad_cross_value = weight_grad(memory_flat, grad_memory_values)
    memory_grad = project_back(grad_memory_keys, cross_key) + project_back(
        grad_memory_values, cross_value
    )
    cross_rows_low = grad_cross_rows.astype(jnp.bfloat16)
    grad_cross_query = weight_grad(hidden_cross, cross_rows_low)
    grad_in_cross, grad_gain_cross, grad_shift_cross = pull_cross(
        project_back(cross_rows_low, cross_query)
    )
    grad_after_self = grad_after_cross + grad_in_cross
    grad_self_low = grad_after_self.astype(jnp.bfloat16)
    grad_self_out = weight_grad(self_mixed, grad_self_low)
    grad_self_mixed = project_back(grad_self_low, self_out).astype(jnp.bfloat16)
    grad_queries, key_terms, value_terms = attend_back(
        query_rows, keys_all, values_all, self_mask, self_total, grad_self_mixed, row_count
    )
    grad_keys, grad_values = (
        lax.psum_scatter(
            key_terms.astype(jnp.bfloat16), "seq", scatter_dimension=1, tiled=True
        ).astype(jnp.float32),
        lax.psum_scatter(
            value_terms.astype(jnp.bfloat16), "seq", scatter_dimension=1, tiled=True
        ).astype(jnp.float32),
    )
    grad_keys = grad_keys.reshape(row_count * shard_len, width).astype(jnp.bfloat16)
    grad_values = grad_values.reshape(row_count * shard_len, width).astype(jnp.bfloat16)
    grad_queries = grad_queries.astype(jnp.bfloat16)
    grad_self_query = weight_grad(hidden_attend, grad_queries)
    grad_self_key = weight_grad(hidden_attend, grad_keys)
    grad_self_value = weight_grad(hidden_attend, grad_values)
    grad_hidden = (
        project_back(grad_queries, self_query)
        + project_back(grad_keys, self_key)
        + project_back(grad_values, self_value)
    )
    grad_in_attend, grad_gain_attend, grad_shift_attend = pull_attend(grad_hidden)
    tokens_grad = grad_after_self + grad_in_attend
    row_parts = (
        lax.psum_scatter(grad_self_query, "dp", scatter_dimension=0, tiled=True),
        lax.psum_scatter(grad_self_key, "dp", scatter_dimension=0, tiled=True),
        lax.psum_scatter(grad_self_value, "dp", scatter_dimension=0, tiled=True),
        lax.psum_scatter(grad_self_out, "dp", scatter_dimension=0, tiled=True),
        lax.psum_scatter(grad_cross_query, "dp", scatter_dimension=0, tiled=True),
        lax.psum_scatter(grad_cross_key, "dp", scatter_dimension=0, tiled=True),
        lax.psum_scatter(grad_cross_value, "dp", scatter_dimension=0, tiled=True),
        lax.psum_scatter(grad_cross_out, "dp", scatter_dimension=0, tiled=True),
        lax.psum_scatter(grad_feed_in, "dp", scatter_dimension=0, tiled=True),
        lax.psum_scatter(grad_feed_out, "dp", scatter_dimension=0, tiled=True),
    )
    column_parts = (
        lax.psum_scatter(
            row_parts[0].astype(jnp.bfloat16), "seq", scatter_dimension=1, tiled=True
        ).astype(jnp.float32),
        lax.psum_scatter(
            row_parts[1].astype(jnp.bfloat16), "seq", scatter_dimension=1, tiled=True
        ).astype(jnp.float32),
        lax.psum_scatter(
            row_parts[2].astype(jnp.bfloat16), "seq", scatter_dimension=1, tiled=True
        ).astype(jnp.float32),
        lax.psum_scatter(
            row_parts[3].astype(jnp.bfloat16), "seq", scatter_dimension=1, tiled=True
        ).astype(jnp.float32),
        lax.psum_scatter(
            row_parts[4].astype(jnp.bfloat16), "seq", scatter_dimension=1, tiled=True
        ).astype(jnp.float32),
        lax.psum_scatter(
            row_parts[5].astype(jnp.bfloat16), "seq", scatter_dimension=1, tiled=True
        ).astype(jnp.float32),
        lax.psum_scatter(
            row_parts[6].astype(jnp.bfloat16), "seq", scatter_dimension=1, tiled=True
        ).astype(jnp.float32),
        lax.psum_scatter(
            row_parts[7].astype(jnp.bfloat16), "seq", scatter_dimension=1, tiled=True
        ).astype(jnp.float32),
        lax.psum_scatter(
            row_parts[8].astype(jnp.bfloat16), "seq", scatter_dimension=1, tiled=True
        ).astype(jnp.float32),
        lax.psum_scatter(
            row_parts[9].astype(jnp.bfloat16), "seq", scatter_dimension=1, tiled=True
        ).astype(jnp.float32),
    )
    weight_totals = (
        lax.all_gather(column_parts[0].astype(jnp.bfloat16), "seq", axis=1, tiled=True).astype(
            jnp.float32
        ),
        lax.all_gather(column_parts[1].astype(jnp.bfloat16), "seq", axis=1, tiled=True).astype(
            jnp.float32
        ),
        lax.all_gather(column_parts[2].astype(jnp.bfloat16), "seq", axis=1, tiled=True).astype(
            jnp.float32
        ),
        lax.all_gather(column_parts[3].astype(jnp.bfloat16), "seq", axis=1, tiled=True).astype(
            jnp.float32
        ),
        lax.all_gather(column_parts[4].astype(jnp.bfloat16), "seq", axis=1, tiled=True).astype(
            jnp.float32
        ),
        lax.all_gather(column_parts[5].astype(jnp.bfloat16), "seq", axis=1, tiled=True).astype(
            jnp.float32
        ),
        lax.all_gather(column_parts[6].astype(jnp.bfloat16), "seq", axis=1, tiled=True).astype(
            jnp.float32
        ),
        lax.all_gather(column_parts[7].astype(jnp.bfloat16), "seq", axis=1, tiled=True).astype(
            jnp.float32
        ),
        lax.all_gather(column_parts[8].astype(jnp.bfloat16), "seq", axis=1, tiled=True).astype(
            jnp.float32
        ),
        lax.all_gather(column_parts[9].astype(jnp.bfloat16), "seq", axis=1, tiled=True).astype(
            jnp.float32
        ),
    )
    stacked = jnp.stack(
        [
            grad_gain_attend,
            grad_shift_attend,
            grad_gain_cross,
            grad_shift_cross,
            grad_gain_feed,
            grad_shift_feed,
        ]
    )
    stacked_total = lax.psum(stacked, ("seq", "dp"))
    share = width // lax.axis_size("dp")
    norm_part = lax.dynamic_slice_in_dim(stacked_total, lax.axis_index("dp") * share, share, 1)
    summed = tuple(weight_totals) + (
        norm_part[0],
        norm_part[1],
        norm_part[2],
        norm_part[3],
        norm_part[4],
        norm_part[5],
    )
    return (
        layer_out.reshape(row_count, shard_len, width),
        tokens_grad.reshape(row_count, shard_len, width),
        memory_grad.reshape(row_count, src_shard, width),
        summed[0],
        summed[1],
        summed[2],
        summed[3],
        summed[4],
        summed[5],
        summed[6],
        summed[7],
        summed[8],
        summed[9],
        summed[10],
        summed[11],
        summed[12],
        summed[13],
        summed[14],
        summed[15],
    )


def solution(mesh):
    in_specs = (
        P("dp", "seq", None),
        P("dp", "seq", None),
        P("dp", None),
        P("dp", None),
        P("dp", None),
        P("dp", "seq", None),
        P(),
        P(),
        P(),
        P(),
        P(),
        P(),
        P(),
        P(),
        P(),
        P(),
        P(),
        P(),
        P(),
        P(),
        P(),
        P(),
    )
    out_specs = (
        P("dp", "seq", None),
        P("dp", "seq", None),
        P("dp", "seq", None),
        P("dp", None),
        P("dp", None),
        P("dp", None),
        P("dp", None),
        P("dp", None),
        P("dp", None),
        P("dp", None),
        P("dp", None),
        P("dp", None),
        P("dp", None),
        P("dp"),
        P("dp"),
        P("dp"),
        P("dp"),
        P("dp"),
        P("dp"),
    )
    return jax.shard_map(shards, mesh=mesh, in_specs=in_specs, out_specs=out_specs, check_vma=False)
```

profile of v0, /device:TPU:0, one launch (start us, length us, event | category | flops | bytes accessed | tf_op | source)
XLA Modules:
  0.0 1360.6 jit_solution(9825368612494991412)
XLA Ops:
  13.4 10.9 all-gather.1
  29.7 10.3 all-gather
  134.0 12.9 reduce-scatter.73.cloned.1.call-done
  150.5 27.0 %reduce-scatter.49.cloned.1.call-done = bf16[1,256,768]{1,2,0:T(8,128)(2,1)} async-done(((bf16[1,1024,768]{1,2,0:T(8,128)(2,1)}), bf16[1,256,768]{1,2,0:T(8,128)(2,1)}) %reduce-scatter.49.cloned.1.call-update) | async-done | bytes 393232 | tf_op jit(solution)/shard_map/reduce_scatter | solution.py:201
  183.5 24.7 %reduce-scatter.47.cloned.1.call-done = bf16[1,256,768]{1,2,0:T(8,128)(2,1)} async-done(((bf16[1,1024,768]{1,2,0:T(8,128)(2,1)}), bf16[1,256,768]{1,2,0:T(8,128)(2,1)}) %reduce-scatter.47.cloned.1.call-update) | async-done | bytes 393232 | tf_op jit(solution)/shard_map/reduce_scatter | solution.py:198
  226.8 53.9 %reduce-scatter.59.cloned.1.call-done = f32[96,768]{1,0:T(8,128)} async-done(((f32[768,768]{1,0:T(8,128)}), f32[96,768]{1,0:T(8,128)}) %reduce-scatter.59.cloned.1.call-update) | async-done | bytes 294928 | tf_op jit(solution)/shard_map/reduce_scatter | solution.py:252
  282.6 69.8 %reduce-scatter.57.cloned.1.call-done = f32[96,768]{1,0:T(8,128)} async-done(((f32[768,768]{1,0:T(8,128)}), f32[96,768]{1,0:T(8,128)}) %reduce-scatter.57.cloned.1.call-update) | async-done | bytes 294928 | tf_op jit(solution)/shard_map/reduce_scatter | solution.py:251
  354.3 69.8 %reduce-scatter.65.cloned.1.call-done = f32[96,768]{1,0:T(8,128)} async-done(((f32[768,768]{1,0:T(8,128)}), f32[96,768]{1,0:T(8,128)}) %reduce-scatter.65.cloned.1.call-update) | async-done | bytes 294928 | tf_op jit(solution)/shard_map/reduce_scatter | solution.py:255
  426.0 69.8 %reduce-scatter.51.cloned.1.call-done = f32[96,768]{1,0:T(8,128)} async-done(((f32[768,768]{1,0:T(8,128)}), f32[96,768]{1,0:T(8,128)}) %reduce-scatter.51.cloned.1.call-update) | async-done | bytes 294928 | tf_op jit(solution)/shard_map/reduce_scatter | solution.py:248
  497.7 69.7 %reduce-scatter.55.cloned.1.call-done = f32[96,768]{1,0:T(8,128)} async-done(((f32[768,768]{1,0:T(8,128)}), f32[96,768]{1,0:T(8,128)}) %reduce-scatter.55.cloned.1.call-update) | async-done | bytes 294928 | tf_op jit(solution)/shard_map/reduce_scatter | solution.py:250
  569.2 69.8 %reduce-scatter.53.cloned.1.call-done = f32[96,768]{1,0:T(8,128)} async-done(((f32[768,768]{1,0:T(8,128)}), f32[96,768]{1,0:T(8,128)}) %reduce-scatter.53.cloned.1.call-update) | async-done | bytes 294928 | tf_op jit(solution)/shard_map/reduce_scatter | solution.py:249
  640.9 69.7 %reduce-scatter.89.cloned.1.call-done = f32[96,768]{1,0:T(8,128)} async-done(((f32[768,768]{1,0:T(8,128)}), f32[96,768]{1,0:T(8,128)}) %reduce-scatter.89.cloned.1.call-update) | async-done | bytes 294928
  716.3 66.0 %reduce-scatter.87.cloned.1.call-done = f32[96,768]{1,0:T(8,128)} async-done(((f32[768,768]{1,0:T(8,128)}), f32[96,768]{1,0:T(8,128)}) %reduce-scatter.87.cloned.1.call-update) | async-done | bytes 294928
  787.9 160.4 %reduce-scatter.67.cloned.1.call-done = f32[96,3072]{1,0:T(8,128)} async-done(((f32[768,3072]{1,0:T(8,128)}), f32[96,3072]{1,0:T(8,128)}) %reduce-scatter.67.cloned.1.call-update) | async-done | bytes 1179664 | tf_op jit(solution)/shard_map/reduce_scatter | solution.py:256
  952.9 42.8 %psum.7 = f32[6,768]{1,0:T(8,128)S(1)} all-reduce(f32[6,768]{1,0:T(8,128)S(1)} %stack.2), channel_id=1, replica_groups=mesh['seq'=4,'dp'=8] {'seq','dp'}, use_global_device_ids=true, to_apply=%region_48.49 | all-reduce | flops 4608 | bytes 36864 | tf_op jit(solution)/shard_map/psum | solution.py:333
  996.7 118.7 %reduce-scatter.71.cloned.1.call-done = f32[384,768]{1,0:T(8,128)} async-done(((f32[3072,768]{1,0:T(8,128)}), f32[384,768]{1,0:T(8,128)}) %reduce-scatter.71.cloned.1.call-update) | async-done | bytes 1179664 | tf_op jit(solution)/shard_map/reduce_scatter | solution.py:257
  1120.6 16.6 %reduce-scatter.85.cloned.1.call-done = bf16[192,96]{1,0:T(8,128)(2,1)} async-done(((bf16[768,96]{1,0:T(8,128)(2,1)}), bf16[192,96]{1,0:T(8,128)(2,1)}) %reduce-scatter.85.cloned.1.call-update) | async-done | bytes 36880
  1137.2 5.8 all_gather.46
  1143.8 16.0 %reduce-scatter.83.cloned.1.call-done = bf16[192,96]{1,0:T(8,128)(2,1)} async-done(((bf16[768,96]{1,0:T(8,128)(2,1)}), bf16[192,96]{1,0:T(8,128)(2,1)}) %reduce-scatter.83.cloned.1.call-update) | async-done | bytes 36880
  1166.5 16.0 %reduce-scatter.91.cloned.1.call-done = bf16[192,96]{1,0:T(8,128)(2,1)} async-done(((bf16[768,96]{1,0:T(8,128)(2,1)}), bf16[192,96]{1,0:T(8,128)(2,1)}) %reduce-scatter.91.cloned.1.call-update) | async-done | bytes 36880
  1189.1 16.1 %reduce-scatter.77.cloned.1.call-done = bf16[192,96]{1,0:T(8,128)(2,1)} async-done(((bf16[768,96]{1,0:T(8,128)(2,1)}), bf16[192,96]{1,0:T(8,128)(2,1)}) %reduce-scatter.77.cloned.1.call-update) | async-done | bytes 36880
  1211.9 16.0 %reduce-scatter.81.cloned.1.call-done = bf16[192,96]{1,0:T(8,128)(2,1)} async-done(((bf16[768,96]{1,0:T(8,128)(2,1)}), bf16[192,96]{1,0:T(8,128)(2,1)}) %reduce-scatter.81.cloned.1.call-update) | async-done | bytes 36880
  1227.9 5.8 all_gather.44
  1234.6 16.1 %reduce-scatter.79.cloned.1.call-done = bf16[192,96]{1,0:T(8,128)(2,1)} async-done(((bf16[768,96]{1,0:T(8,128)(2,1)}), bf16[192,96]{1,0:T(8,128)(2,1)}) %reduce-scatter.79.cloned.1.call-update) | async-done | bytes 36880
  1250.7 5.8 all_gather.43
  1257.4 15.6 %reduce-scatter.63.cloned.1.call-done = bf16[96,192]{0,1:T(8,128)(2,1)} async-done(((bf16[96,768]{0,1:T(8,128)(2,1)}), bf16[96,192]{0,1:T(8,128)(2,1)}) %reduce-scatter.63.cloned.1.call-update) | async-done | bytes 36880 | tf_op jit(solution)/shard_map/reduce_scatter | solution.py:278
  1279.6 16.1 %reduce-scatter.61.cloned.1.call-done = bf16[96,192]{0,1:T(8,128)(2,1)} async-done(((bf16[96,768]{0,1:T(8,128)(2,1)}), bf16[96,192]{0,1:T(8,128)(2,1)}) %reduce-scatter.61.cloned.1.call-update) | async-done | bytes 36880 | tf_op jit(solution)/shard_map/reduce_scatter | solution.py:275
  1295.7 5.8 all_gather.47
  1302.4 18.4 %reduce-scatter.69.cloned.1.call-done = bf16[96,768]{1,0:T(8,128)(2,1)} async-done(((bf16[96,3072]{1,0:T(8,128)(2,1)}), bf16[96,768]{1,0:T(8,128)(2,1)}) %reduce-scatter.69.cloned.1.call-update) | async-done | bytes 147472 | tf_op jit(solution)/shard_map/reduce_scatter | solution.py:284
  1320.7 7.3 all_gather.50
  1329.2 16.1 %reduce-scatter.93.cloned.1.call-done = bf16[192,384]{1,0:T(8,128)(2,1)} async-done(((bf16[768,384]{1,0:T(8,128)(2,1)}), bf16[192,384]{1,0:T(8,128)(2,1)}) %reduce-scatter.93.cloned.1.call-update) | async-done | bytes 147472
  1345.3 7.3 all_gather.51
  (384 shorter events, 196.4 us)
Async XLA Ops:
  7.2 41.7 %copy-start = (bf16[768,768]{1,0:T(8,128)(2,1)S(1)}, bf16[768,768]{1,0:T(8,128)(2,1)}, u32[]{:S(2)}) copy-start(bf16[768,768]{1,0:T(8,128)(2,1)} %param.33) | copy-start | bytes 3538948
  7.2 41.7 %all-gather.4.cloned.1.call-start = ((), (), s32[]{:S(2)}) async-start(), calls=%async_computation.24 | async-start | bytes 1966080 | tf_op jit(solution)/shard_map/all_gather | solution.py:166
  7.9 122.4 %reduce-scatter.75.cloned.1.call-start = ((), (), s32[]{:S(2)}) async-start(), calls=%async_computation.39 | async-start | bytes 983040
  95.4 51.4 %reduce-scatter.73.cloned.1.call-start = ((), (), s32[]{:S(2)}) async-start(), calls=%async_computation.38 | async-start | bytes 983040
  106.4 71.1 %reduce-scatter.49.cloned.1.call-start = ((), (), s32[]{:S(2)}) async-start(), calls=%async_computation.26 | async-start | bytes 1966080 | tf_op jit(solution)/shard_map/reduce_scatter | solution.py:201
  111.7 96.5 %reduce-scatter.47.cloned.1.call-start = ((), (), s32[]{:S(2)}) async-start(), calls=%async_computation.25 | async-start | bytes 1966080 | tf_op jit(solution)/shard_map/reduce_scatter | solution.py:198
  116.3 164.4 %reduce-scatter.59.cloned.1.call-start = ((), (), s32[]{:S(2)}) async-start(), calls=%async_computation.31 | async-start | bytes 2654208 | tf_op jit(solution)/shard_map/reduce_scatter | solution.py:252
  119.2 233.2 %reduce-scatter.57.cloned.1.call-start = ((), (), s32[]{:S(2)}) async-start(), calls=%async_computation.30 | async-start | bytes 2654208 | tf_op jit(solution)/shard_map/reduce_scatter | solution.py:251
  122.1 302.0 %reduce-scatter.65.cloned.1.call-start = ((), (), s32[]{:S(2)}) async-start(), calls=%async_computation.34 | async-start | bytes 2654208 | tf_op jit(solution)/shard_map/reduce_scatter | solution.py:255
  125.0 370.8 %reduce-scatter.51.cloned.1.call-start = ((), (), s32[]{:S(2)}) async-start(), calls=%async_computation.27 | async-start | bytes 2654208 | tf_op jit(solution)/shard_map/reduce_scatter | solution.py:248
  130.3 437.1 %reduce-scatter.55.cloned.1.call-start = ((), (), s32[]{:S(2)}) async-start(), calls=%async_computation.29 | async-start | bytes 2654208 | tf_op jit(solution)/shard_map/reduce_scatter | solution.py:250
  134.0 505.1 %reduce-scatter.53.cloned.1.call-start = ((), (), s32[]{:S(2)}) async-start(), calls=%async_computation.28 | async-start | bytes 2654208 | tf_op jit(solution)/shard_map/reduce_scatter | solution.py:249
  150.4 560.2 %reduce-scatter.89.cloned.1.call-start = ((), (), s32[]{:S(2)}) async-start(), calls=%async_computation.46 | async-start | bytes 2654208
  183.4 598.9 %reduce-scatter.87.cloned.1.call-start = ((), (), s32[]{:S(2)}) async-start(), calls=%async_computation.45 | async-start | bytes 2654208
  214.2 734.1 %reduce-scatter.67.cloned.1.call-start = ((), (), s32[]{:S(2)}) async-start(), calls=%async_computation.35 | async-start | bytes 10616832 | tf_op jit(solution)/shard_map/reduce_scatter | solution.py:256
  220.5 894.9 %reduce-scatter.71.cloned.1.call-start = ((), (), s32[]{:S(2)}) async-start(), calls=%async_computation.37 | async-start | bytes 10616832 | tf_op jit(solution)/shard_map/reduce_scatter | solution.py:257
  226.7 910.4 %reduce-scatter.85.cloned.1.call-start = ((), (), s32[]{:S(2)}) async-start(), calls=%async_computation.44 | async-start | bytes 245760
  282.5 877.3 %reduce-scatter.83.cloned.1.call-start = ((), (), s32[]{:S(2)}) async-start(), calls=%async_computation.43 | async-start | bytes 245760
  354.2 828.3 %reduce-scatter.91.cloned.1.call-start = ((), (), s32[]{:S(2)}) async-start(), calls=%async_computation.47 | async-start | bytes 245760
  425.9 779.3 %reduce-scatter.77.cloned.1.call-start = ((), (), s32[]{:S(2)}) async-start(), calls=%async_computation.40 | async-start | bytes 245760
  497.6 730.3 %reduce-scatter.81.cloned.1.call-start = ((), (), s32[]{:S(2)}) async-start(), calls=%async_computation.42 | async-start | bytes 245760
  569.2 681.5 %reduce-scatter.79.cloned.1.call-start = ((), (), s32[]{:S(2)}) async-start(), calls=%async_computation.41 | async-start | bytes 245760
  640.9 632.0 %reduce-scatter.63.cloned.1.call-start = ((), (), s32[]{:S(2)}) async-start(), calls=%async_computation.33 | async-start | bytes 245760 | tf_op jit(solution)/shard_map/reduce_scatter | solution.py:278
  712.4 583.3 %reduce-scatter.61.cloned.1.call-start = ((), (), s32[]{:S(2)}) async-start(), calls=%async_computation.32 | async-start | bytes 245760 | tf_op jit(solution)/shard_map/reduce_scatter | solution.py:275
  716.3 69.7 %copy-start.60 = (f32[768]{0:T(1024)S(1)}, f32[768]{0:T(1024)}, u32[]{:S(2)}) copy-start(f32[768]{0:T(1024)} %get-tuple-element.78) | copy-start | bytes 9220
  716.3 69.7 %copy-start.59 = (f32[768]{0:T(1024)S(1)}, f32[768]{0:T(1024)}, u32[]{:S(2)}) copy-start(f32[768]{0:T(1024)} %get-tuple-element.83) | copy-start | bytes 9220
  716.3 69.7 %copy-start.58 = (f32[768]{0:T(1024)S(1)}, f32[768]{0:T(1024)}, u32[]{:S(2)}) copy-start(f32[768]{0:T(1024)} %get-tuple-element.76) | copy-start | bytes 9220
  716.3 69.7 %copy-start.57 = (f32[768]{0:T(1024)S(1)}, f32[768]{0:T(1024)}, u32[]{:S(2)}) copy-start(f32[768]{0:T(1024)} %get-tuple-element.82) | copy-start | bytes 9220
  784.1 536.6 %reduce-scatter.69.cloned.1.call-start = ((), (), s32[]{:S(2)}) async-start(), calls=%async_computation.36 | async-start | bytes 737280 | tf_op jit(solution)/shard_map/reduce_scatter | solution.py:284
  950.5 45.2 %copy-start.12 = (f32[128,768]{1,0:T(8,128)S(1)}, f32[128,768]{1,0:T(8,128)}, u32[]{:S(2)}) copy-start(f32[128,768]{1,0:T(8,128)} %copy-done.11) | copy-start | bytes 1179652
  950.5 394.8 %reduce-scatter.93.cloned.1.call-start = ((), (), s32[]{:S(2)}) async-start(), calls=%async_computation.48 | async-start | bytes 737280
  996.7 121.7 %copy-start.37 = (bf16[1,256,768]{1,2,0:T(8,128)(2,1)S(1)}, bf16[1,256,768]{1,2,0:T(8,128)(2,1)}, u32[]{:S(2)}) copy-start(bf16[1,256,768]{1,2,0:T(8,128)(2,1)} %reduce-scatter.47.cloned.1.call-done) | copy-start | bytes 1179652
  (88 other events, 394.4 us)
Sparse Core Ops, SparseCore 0:
  9.6 22.9 all-gather.3
  95.6 24.7 reduce-scatter.74
  123.6 23.2 reduce-scatter.72
  149.3 28.1 reduce-scatter.48
  180.0 28.1 reduce-scatter.46
  211.5 69.1 reduce-scatter.58
  284.2 68.1 reduce-scatter.56
  355.9 68.1 reduce-scatter.64
  427.6 68.1 reduce-scatter.50
  499.1 68.1 reduce-scatter.54
  570.9 68.1 reduce-scatter.52
  642.4 68.1 reduce-scatter.88
  714.1 68.1 reduce-scatter.86
  785.8 162.4 reduce-scatter.66
  951.8 163.6 reduce-scatter.70
  1118.3 18.8 reduce-scatter.84
  1140.0 19.7 reduce-scatter.82
  1162.7 19.7 reduce-scatter.90
  1185.5 19.7 reduce-scatter.76
  1208.1 19.7 reduce-scatter.80
  1230.9 19.7 reduce-scatter.78
  1253.1 19.7 reduce-scatter.62
  1275.9 19.7 reduce-scatter.60
  1298.7 22.0 reduce-scatter.68
  1323.2 22.0 reduce-scatter.92
where the time goes:
time: 1370 us; the launch traced here: 1360 us
  waiting for transfers between devices  1050 us (77%)
  blocking collectives  125 us (9%)
  matrix products  90.8 us (7%)
  local copies, waits for them, and re-layouts  57.8 us (4%)
  other arithmetic  22.3 us (2%)
  between operations  17.1 us (1%)
    unnamed x36, waiting for transfers between devices  263 us
    reduce_scatter x1, waiting for transfers between devices, shards(): lax.psum_scatter(grad_feed_in, 'dp', scatter_dimension=0, tiled=True)  160 us
    reduce_scatter x1, waiting for transfers between devices, shards(): lax.psum_scatter(grad_feed_out, 'dp', scatter_dimension=0, tiled=True)  119 us
    reduce_scatter x1, waiting for transfers between devices, shards(): lax.psum_scatter(grad_self_key, 'dp', scatter_dimension=0, tiled=True)  69.8 us
    reduce_scatter x1, waiting for transfers between devices, shards(): lax.psum_scatter(grad_self_query, 'dp', scatter_dimension=0, tiled=True)  69.8 us
    reduce_scatter x1, waiting for transfers between devices, shards(): lax.psum_scatter(grad_cross_out, 'dp', scatter_dimension=0, tiled=True)  69.8 us
    reduce_scatter x1, waiting for transfers between devices, shards(): lax.psum_scatter(grad_self_out, 'dp', scatter_dimension=0, tiled=True)  69.8 us
    reduce_scatter x1, waiting for transfers between devices, shards(): lax.psum_scatter(grad_self_value, 'dp', scatter_dimension=0, tiled=True)  69.7 us
  transfers between devices with their start and end apart: 25, of which 23 were waited for; matrix products, arithmetic and copies ran while one was open for 8% of the time, Pallas kernels for 0%

commit v1 on v0

v1 whole, which is shorter than its diff:
```python
import jax
import jax.numpy as jnp
from jax import lax
from jax.sharding import PartitionSpec as P

HEAD_DIM = 64
EPSILON = 1e-05
NEGATIVE = -1e30
F32 = jnp.float32
BF16 = jnp.bfloat16


def normalize(values):
    centered = values - jnp.mean(values, axis=-1, keepdims=True)
    rate = lax.rsqrt(jnp.mean(centered * centered, axis=-1, keepdims=True) + EPSILON)
    return centered * rate, rate


def norm_back(grad, gain, normed, rate):
    scaled = grad * gain
    inner = jnp.mean(scaled * normed, axis=-1, keepdims=True)
    return rate * (scaled - jnp.mean(scaled, axis=-1, keepdims=True) - normed * inner)


def mm(left, right):
    return jnp.dot(left, right, preferred_element_type=F32)


def mm_t(left, right):
    return lax.dot_general(left, right, (((1,), (1,)), ((), ())), preferred_element_type=F32)


def t_mm(left, right):
    return lax.dot_general(left, right, (((0,), (0,)), ((), ())), preferred_element_type=F32)


def heads(values):
    return values.reshape(values.shape[0], -1, HEAD_DIM)


def scores_of(query, key, allowed):
    scores = jnp.einsum("qhd,khd->hqk", query, key, preferred_element_type=F32) * HEAD_DIM**-0.5
    return jnp.where(allowed[None], scores, NEGATIVE)


def attend(query, key, value, allowed):
    scores = scores_of(heads(query), heads(key), allowed)
    highest = jnp.max(scores, axis=-1, keepdims=True)
    exponent = jnp.exp(scores - highest)
    totals = jnp.sum(exponent, axis=-1, keepdims=True)
    weights = (exponent / totals).astype(BF16)
    mixed = jnp.einsum("hqk,khd->qhd", weights, heads(value), preferred_element_type=F32)
    return mixed.reshape(query.shape).astype(BF16), highest + jnp.log(totals)


def attend_back(query, key, value, allowed, log_total, grad):
    query, key, value, grad = heads(query), heads(key), heads(value), heads(grad)
    weights = jnp.exp(scores_of(query, key, allowed) - log_total)
    grad_weights = jnp.einsum("qhd,khd->hqk", grad, value, preferred_element_type=F32)
    inner = jnp.sum(weights * grad_weights, axis=-1, keepdims=True)
    grad_scores = (weights * (grad_weights - inner)).astype(BF16)
    factor = HEAD_DIM**-0.5
    grad_query = jnp.einsum("hqk,khd->qhd", grad_scores, key, preferred_element_type=F32) * factor
    grad_key = jnp.einsum("hqk,qhd->khd", grad_scores, query, preferred_element_type=F32) * factor
    grad_value = jnp.einsum("hqk,qhd->khd", weights.astype(BF16), grad, preferred_element_type=F32)
    flat = lambda v: v.reshape(v.shape[0], -1).astype(BF16)
    return flat(grad_query), flat(grad_key), flat(grad_value)


def swap(value, axis, bit):
    size = lax.axis_size(axis)
    return lax.ppermute(value, axis, [(i, i ^ bit) for i in range(size)])


def scatter_sum(value, bits):
    index = lax.axis_index("dp")
    size = lax.axis_size("dp")
    levels = size.bit_length() - 1
    blocks = value.reshape((2,) * levels + value.shape[1:])
    left = list(range(levels))[::-1]
    for bit in bits:
        place = left.index(bit)
        mine = (index >> bit) & 1
        keep = lax.dynamic_index_in_dim(blocks, mine, place, keepdims=False)
        send = lax.dynamic_index_in_dim(blocks, 1 - mine, place, keepdims=False)
        left.pop(place)
        got = swap(send.astype(BF16), "dp", 1 << bit)
        blocks = keep.astype(F32) + got.astype(F32)
    return blocks


def shards(
    tokens,
    memory,
    target_segments,
    memory_segments,
    pad_counts,
    out_grad,
    self_query,
    self_key,
    self_value,
    self_out,
    cross_query,
    cross_key,
    cross_value,
    cross_out,
    feed_in,
    feed_out,
    gain_attend,
    shift_attend,
    gain_cross,
    shift_cross,
    gain_feed,
    shift_feed,
):
    seq, dp = lax.axis_size("seq"), lax.axis_size("dp")
    me = lax.axis_index("seq")
    span, width = tokens.shape[1:]
    full, src_full = span * seq, memory.shape[1] * seq
    part = width // seq
    feed = feed_in.shape[1]
    unit = feed // dp // seq

    def columns(weight):
        return lax.dynamic_slice_in_dim(weight, me * part, part, 1)

    def rows(weight):
        return lax.dynamic_slice_in_dim(weight, me * part, part, 0)

    def own(values):
        return lax.dynamic_slice_in_dim(values, me * span, span, 0)

    fi = lax.dynamic_index_in_dim(
        feed_in.reshape(width, dp, seq, unit), me, 2, keepdims=False
    ).reshape(width, dp * unit)
    fo = lax.dynamic_index_in_dim(
        feed_out.reshape(dp, seq, unit, width), me, 1, keepdims=False
    ).reshape(dp * unit, width)

    gather = lambda v, axis: lax.all_gather(v, "seq", axis=axis, tiled=True)
    scatter = lambda v: lax.psum_scatter(
        v.astype(BF16), "seq", scatter_dimension=0, tiled=True
    ).astype(F32)

    target_ids, memory_ids = target_segments[0], memory_segments[0]
    places = jnp.arange(full)
    same = target_ids[None, :] == target_ids[:, None]
    alive = (places < full - pad_counts[0, 0])[None, :] | (places[None, :] == places[:, None])
    self_mask = same & (places[None, :] <= places[:, None]) & alive
    cross_mask = (memory_ids[None, :] == target_ids[:, None]) & (
        jnp.arange(src_full) < src_full - pad_counts[0, 1]
    )[None, :]

    row = gather(tokens[0], 0).astype(F32)
    source = gather(memory[0], 0)
    grad_out = gather(out_grad[0], 0)

    gains = [g.astype(F32) for g in (gain_attend, gain_cross, gain_feed)]
    shifts = [g.astype(F32) for g in (shift_attend, shift_cross, shift_feed)]

    n_attend, r_attend = normalize(row)
    h_attend = (n_attend * gains[0] + shifts[0]).astype(BF16)
    query = mm(h_attend, columns(self_query)).astype(BF16)
    key = mm(h_attend, columns(self_key)).astype(BF16)
    value = mm(h_attend, columns(self_value)).astype(BF16)
    mixed_own, self_total = attend(query, key, value, self_mask)
    self_mixed = gather(mixed_own, 1)
    after_self = row + mm(self_mixed, self_out)
    n_cross, r_cross = normalize(after_self)
    h_cross = (n_cross * gains[1] + shifts[1]).astype(BF16)
    cross_rows = mm(h_cross, columns(cross_query)).astype(BF16)
    mem_keys = mm(source, columns(cross_key)).astype(BF16)
    mem_values = mm(source, columns(cross_value)).astype(BF16)
    cross_own, cross_total = attend(cross_rows, mem_keys, mem_values, cross_mask)
    cross_mixed = gather(cross_own, 1)
    after_cross = after_self + mm(cross_mixed, cross_out)
    n_feed, r_feed = normalize(after_cross)
    h_feed = (n_feed * gains[2] + shifts[2]).astype(BF16)
    upward = mm(h_feed, fi)
    activated, pull_gelu = jax.vjp(lambda v: jax.nn.gelu(v, approximate=False), upward)
    activated = activated.astype(BF16)
    layer_out = own(after_cross) + scatter(mm(activated, fo))

    grad_upward = pull_gelu(mm_t(grad_out, fo))[0].astype(BF16)
    grad_fo = t_mm(activated, grad_out)
    grad_fi = t_mm(h_feed, grad_upward)
    grad_h = gather(scatter(mm_t(grad_upward, fi)).astype(BF16), 0).astype(F32)
    stats = [None] * 6
    stats[4], stats[5] = jnp.sum(grad_h * n_feed, 0), jnp.sum(grad_h, 0)
    grad_after_cross = grad_out.astype(F32) + norm_back(grad_h, gains[2], n_feed, r_feed)
    gac = grad_after_cross.astype(BF16)
    grad_co = t_mm(cross_mixed, columns(gac))
    grad_cm = mm_t(gac, rows(cross_out)).astype(BF16)
    grad_cr, grad_mk, grad_mv = attend_back(
        cross_rows, mem_keys, mem_values, cross_mask, cross_total, grad_cm
    )
    grad_ck, grad_cv = t_mm(source, grad_mk), t_mm(source, grad_mv)
    memory_grad = scatter(mm_t(grad_mk, columns(cross_key)) + mm_t(grad_mv, columns(cross_value)))
    grad_cq = t_mm(h_cross, grad_cr)
    grad_h = mm_t(gather(grad_cr, 1), cross_query)
    stats[2], stats[3] = jnp.sum(grad_h * n_cross, 0), jnp.sum(grad_h, 0)
    grad_after_self = grad_after_cross + norm_back(grad_h, gains[1], n_cross, r_cross)
    gas = grad_after_self.astype(BF16)
    grad_so = t_mm(self_mixed, columns(gas))
    grad_sm = mm_t(gas, rows(self_out)).astype(BF16)
    grad_q, grad_k, grad_v = attend_back(query, key, value, self_mask, self_total, grad_sm)
    grad_h = scatter(
        mm_t(grad_q, columns(self_query))
        + mm_t(grad_k, columns(self_key))
        + mm_t(grad_v, columns(self_value))
    )
    grad_sq, grad_sk, grad_sv = (t_mm(h_attend, g) for g in (grad_q, grad_k, grad_v))
    n_own = own(n_attend)
    stats[0], stats[1] = jnp.sum(grad_h * n_own, 0), jnp.sum(grad_h, 0)
    tokens_grad = own(grad_after_self) + norm_back(grad_h, gains[0], n_own, own(r_attend))

    levels = dp.bit_length() - 1
    up = list(range(levels))
    first, second = up, up[1:] + up[:1]
    share = width // dp
    split = lambda v: v.reshape(dp, share, -1)
    groups = (
        (split(grad_fo), first),
        (split(grad_fi), second),
        (split(jnp.concatenate([grad_co, grad_ck, grad_cv, grad_cq], 1)), first),
        (split(jnp.concatenate([grad_so, grad_sq, grad_sk, grad_sv], 1)), second),
    )
    summed = [gather(scatter_sum(v, bits).astype(BF16)[None], 0) for v, bits in groups]
    whole_fo = summed[0].reshape(seq * share, width).astype(F32)
    whole_fi = (
        summed[1].reshape(seq, share, dp, unit).transpose(1, 2, 0, 3).reshape(share, feed)
    ).astype(F32)

    def whole(group, at):
        block = group[:, :, at * part : (at + 1) * part]
        return block.transpose(1, 0, 2).reshape(share, width).astype(F32)

    co, ck, cv, cq = (whole(summed[2], at) for at in range(4))
    so, sq, sk, sv = (whole(summed[3], at) for at in range(4))

    shared = (me == 0).astype(F32)
    stats = jnp.stack(stats[:2] + [v * shared for v in stats[2:]])
    stats = lax.psum(stats, ("seq", "dp"))
    norm_part = lax.dynamic_slice_in_dim(stats, lax.axis_index("dp") * share, share, 1)
    return (
        layer_out[None],
        tokens_grad[None],
        memory_grad[None],
        sq,
        sk,
        sv,
        so,
        cq,
        ck,
        cv,
        co,
        whole_fi,
        whole_fo,
    ) + tuple(norm_part[i] for i in range(6))


def solution(mesh):
    rows = P("dp", "seq", None)
    in_specs = (rows, rows, P("dp", None), P("dp", None), P("dp", None), rows) + (P(),) * 16
    out_specs = (rows,) * 3 + (P("dp", None),) * 10 + (P("dp"),) * 6
    return jax.shard_map(shards, mesh=mesh, in_specs=in_specs, out_specs=out_specs, check_vma=False)
```

time: 1370 us -> 364 us (0.27)
  waiting for transfers between devices: 1050 us -> 46.6 us
  matrix products: 90.8 us -> 61.6 us
  starting transfers between devices: 1.21 us -> 16.5 us
    reduce_scatter x13 -> x4, waiting for transfers between devices: 784 us -> 0.03 us  [shards(): lax.psum_scatter(v.astype(BF16), 'seq', scatter_dimension=0, tiled=True)]
    unnamed x36 -> x5, waiting for transfers between devices: 263 us -> 0.75 us
    ppermute x0 -> x12, waiting for transfers between devices: none -> 45.8 us  [swap(): return lax.ppermute(value, axis, [(i, i ^ bit) for i in range(size)])]
    unnamed x218 -> x177, local copies, waits for them, and re-layouts: 52.6 us -> 13.6 us
    dot_general x42, matrix products: 90.8 us -> 61.6 us  [the longest x10 20.4 us: mm(): return jnp.dot(left, right, preferred_element_type=F32)]
    convert_element_type x4 -> x31, local copies, waits for them, and re-layouts: 2.22 us -> 24.7 us  [the longest x16 11.5 us: whole(): return block.transpose(1, 0, 2).reshape(share, width).astype(F32)]
    ppermute x0 -> x12, starting transfers between devices: none -> 16.1 us  [swap(): return lax.ppermute(value, axis, [(i, i ^ bit) for i in range(size)])]
    all_gather x12 -> x10, blocking collectives: 82.3 us -> 91.8 us  [shards(): gather = lambda v, axis: lax.all_gather(v, 'seq', axis=axis, tiled=True)]
  transfers between devices with their start and end apart: 25 -> 17, of which waited for: 23 -> 7; matrix products, arithmetic and copies ran while one was open for 8% -> 33% of each run, Pallas kernels for 0% -> 0%
where the time goes in v1:
time: 364 us; the launch traced here: 357 us
  blocking collectives  131 us (36%)
  matrix products  61.6 us (17%)
  local copies, waits for them, and re-layouts  50.9 us (14%)
  waiting for transfers between devices  46.6 us (13%)
  other arithmetic  34 us (9%)
  between operations  17 us (5%)
  starting transfers between devices  16.5 us (5%)
    all_gather x10, blocking collectives, shards(): gather = lambda v, axis: lax.all_gather(v, 'seq', axis=axis, tiled=True)  91.8 us
    ppermute x12, waiting for transfers between devices, swap(): return lax.ppermute(value, axis, [(i, i ^ bit) for i in range(size)])  45.8 us
    psum x1, blocking collectives, shards(): stats = lax.psum(stats, ('seq', 'dp'))  38.8 us
    dot_general x10, matrix products, mm(): return jnp.dot(left, right, preferred_element_type=F32)  20.4 us
    dot_general x10, matrix products, mm_t(): lax.dot_general(left, right, (((1,), (1,)), ((), ())), preferred_element_...  18.2 us
    ppermute x12, starting transfers between devices, swap(): return lax.ppermute(value, axis, [(i, i ^ bit) for i in range(size)])  16.1 us
    unnamed x177, local copies, waits for them, and re-layouts  13.6 us
    convert_element_type x16, local copies, waits for them, and re-layouts, whole(): return block.transpose(1, 0, 2).reshape(share, width).astype(F32)  11.5 us
  transfers between devices with their start and end apart: 17, of which 7 were waited for; matrix products, arithmetic and copies ran while one was open for 33% of the time, Pallas kernels for 0%

profile of v1, /device:TPU:0, one launch (start us, length us, event | category | flops | bytes accessed | tf_op | source)
XLA Modules:
  0.0 357.1 jit_solution(8548507730476284555)
XLA Ops:
  11.3 10.2 %all-gather = bf16[1,512,768]{2,1,0:T(8,128)(2,1)S(1)} all-gather(bf16[1,128,768]{2,1,0:T(8,128)(2,1)} %param.22), channel_id=2, replica_groups=mesh['seq'=4,'dp'=8] {'seq'}, dimensions={1}, use_global_device_ids=true | all-gather | bytes 983040 | tf_op jit(solution)/shard_map/all_gather | solution.py:140
  29.1 6.7 %copy.69 = bf16[768,3072]{0,1:T(8,128)(2,1)} copy(bf16[768,3072]{1,0:T(8,128)(2,1)} %param.36) | data formatting | bytes 9437184 | tf_op args[14]
  35.8 2.4 constant_dynamic-slice_fusion.3
  38.2 2.4 constant_dynamic-slice_fusion.4
  45.4 8.7 %all_gather.34 = bf16[512,768]{0,1:T(8,128)(2,1)S(1)} all-gather(bf16[512,192]{0,1:T(8,128)(2,1)S(1)} %bitcast.309), channel_id=1, replica_groups=mesh['seq'=4,'dp'=8] {'seq'}, dimensions={1}, use_global_device_ids=true | all-gather | bytes 983040 | tf_op jit(solution)/shard_map/all_gather | solution.py:140
  58.5 9.2 %all-gather.2 = bf16[1,512,768]{2,1,0:T(8,128)(2,1)S(1)} all-gather(bf16[1,128,768]{2,1,0:T(8,128)(2,1)S(1)} %copy-done.49), channel_id=4, replica_groups=mesh['seq'=4,'dp'=8] {'seq'}, dimensions={1}, use_global_device_ids=true | all-gather | bytes 983040 | tf_op jit(solution)/shard_map/all_gather | solution.py:140
  67.7 2.6 fusion.56
  78.2 8.7 %all_gather.36 = bf16[512,768]{0,1:T(8,128)(2,1)S(1)} all-gather(bf16[512,192]{0,1:T(8,128)(2,1)S(1)} %bitcast.310), channel_id=1, replica_groups=mesh['seq'=4,'dp'=8] {'seq'}, dimensions={1}, use_global_device_ids=true | all-gather | bytes 983040 | tf_op jit(solution)/shard_map/all_gather | solution.py:140
  89.8 5.0 %multiply_convert_fusion.2 = (bf16[512,768]{1,0:T(8,128)(2,1)}, f32[512,768]{1,0:T(8,128)S(1)}, f32[512,768]{1,0:T(8,128)S(1)}) fusion(bf16[768,768]{0,1:T(8,128)(2,1)S(1)} %bitcast.304, f32[512,768]{1,0:T(8,128)S(1)} %get-tuple-element.62, f32[768]{0:T(1024)S(1)} %copy-done.77, f32[768]{0:T(1024)S(1)} %convert_element_type.425, f32[512]{0:T(512)S(1)} %add_rsqrt_fusion, ...), kind=kOutput, calls=%fused_computation.67 | convolution fusion | flops 631504896 | bytes 6694912 | tf_op jit(solution)/shard_map/dot_general | solution.py:26
  99.5 2.2 fusion.136
  109.9 8.6 %collective-permute-done.6 = bf16[2,2,96,768]{3,2,1,0:T(8,128)(2,1)} collective-permute-done((bf16[2,2,96,768]{3,2,1,0:T(8,128)(2,1)}, bf16[2,2,96,768]{3,2,1,0:T(8,128)(2,1)}, u32[]{:S(2)}, u32[]{:S(2)}) %collective-permute-start.6) | collective-permute-done | bytes 589856 | tf_op jit(solution)/shard_map/ppermute | solution.py:72
  120.2 2.6 collective-permute-start.7
  125.7 10.3 %collective-permute-done.7 = bf16[2,96,768]{2,1,0:T(8,128)(2,1)S(1)} collective-permute-done((bf16[2,96,768]{2,1,0:T(8,128)(2,1)S(1)}, bf16[2,96,768]{2,1,0:T(8,128)(2,1)S(1)}, u32[]{:S(2)}, u32[]{:S(2)}) %collective-permute-start.7) | collective-permute-done | bytes 294944 | tf_op jit(solution)/shard_map/ppermute | solution.py:72
  138.9 2.5 collective-permute-done.8
  141.3 10.7 %all-gather.5 = bf16[384,768]{1,0:T(8,128)(2,1)S(1)} all-gather(bf16[96,768]{1,0:T(8,128)(2,1)S(1)} %fusion.108), channel_id=7, replica_groups=mesh['seq'=4,'dp'=8] {'seq'}, dimensions={0}, use_global_device_ids=true | all-gather | bytes 737280 | tf_op jit(solution)/shard_map/all_gather | solution.py:140
  152.1 7.7 %all-gather.6 = bf16[384,768]{1,0:T(8,128)(2,1)S(1)} all-gather(bf16[96,768]{1,0:T(8,128)(2,1)S(1)} %fusion.107), channel_id=8, replica_groups=mesh['seq'=4,'dp'=8] {'seq'}, dimensions={0}, use_global_device_ids=true | all-gather | bytes 737280 | tf_op jit(solution)/shard_map/all_gather | solution.py:140
  163.8 3.8 %reshape.430 = f32[96,3072]{1,0:T(8,128)} reshape(f32[96,8,4,96]{3,2,1,0:T(4,128)} %bitcast.271) | data formatting | bytes 2359296 | tf_op jit(solution)/shard_map/convert_element_type | solution.py:232
  167.6 9.1 %all_gather.38 = bf16[512,768]{1,0:T(8,128)(2,1)S(1)} all-gather(bf16[128,768]{1,0:T(8,128)(2,1)} %reduce-scatter.7.cloned.1.call-done), channel_id=1, replica_groups=mesh['seq'=4,'dp'=8] {'seq'}, dimensions={0}, use_global_device_ids=true | all-gather | bytes 983040 | tf_op jit(solution)/shard_map/all_gather | solution.py:140
  176.7 2.8 fusion.21
  189.6 8.9 %all_gather.39 = bf16[512,768]{0,1:T(8,128)(2,1)S(1)} all-gather(bf16[512,192]{0,1:T(8,128)(2,1)S(1)} %bitcast.285), channel_id=1, replica_groups=mesh['seq'=4,'dp'=8] {'seq'}, dimensions={1}, use_global_device_ids=true | all-gather | bytes 983040 | tf_op jit(solution)/shard_map/all_gather | solution.py:140
  206.4 2.3 multiply_reduce_fusion.1
  211.8 2.2 fusion.77
  217.6 3.7 %multiply_convert_fusion.1 = bf16[3,512,512]{1,2,0:T(8,128)(2,1)S(1)} fusion(f32[3,512,512]{1,2,0:T(8,128)} %get-tuple-element.68, f32[3,512,512]{1,2,0:T(8,128)} %copy-done.2, f32[3,512]{1,0:T(4,128)S(1)} %get-tuple-element.67, f32[3,512]{1,0:T(4,128)S(1)} %log_add_fusion), kind=kLoop, calls=%fused_computation.10 | loop fusion | flops 3145728 | bytes 7876608 | tf_op jit(solution)/shard_map/convert_element_type | solution.py:61
  225.8 2.5 add_convert_fusion.1
  232.4 2.2 fusion.76
  237.6 3.0 add_convert_fusion
  245.1 6.0 %collective-permute-done = bf16[2,2,96,768]{3,2,1,0:T(8,128)(2,1)} collective-permute-done((bf16[2,2,96,768]{3,2,1,0:T(8,128)(2,1)}, bf16[2,2,96,768]{3,2,1,0:T(8,128)(2,1)}, u32[]{:S(2)}, u32[]{:S(2)}) %collective-permute-start) | collective-permute-done | bytes 589856 | tf_op jit(solution)/shard_map/ppermute | solution.py:72
  254.4 6.0 %collective-permute-done.4 = bf16[2,96,768]{2,1,0:T(8,128)(2,1)S(1)} collective-permute-done((bf16[2,96,768]{2,1,0:T(8,128)(2,1)S(1)}, bf16[2,96,768]{2,1,0:T(8,128)(2,1)S(1)}, u32[]{:S(2)}, u32[]{:S(2)}) %collective-permute-start.4) | collective-permute-done | bytes 294944 | tf_op jit(solution)/shard_map/ppermute | solution.py:72
  260.6 11.3 %collective-permute-done.1 = bf16[2,96,768]{2,1,0:T(8,128)(2,1)S(1)} collective-permute-done((bf16[2,96,768]{2,1,0:T(8,128)(2,1)S(1)}, bf16[2,96,768]{2,1,0:T(8,128)(2,1)S(1)}, u32[]{:S(2)}, u32[]{:S(2)}) %collective-permute-start.1) | collective-permute-done | bytes 294944 | tf_op jit(solution)/shard_map/ppermute | solution.py:72
  273.5 10.9 %all-gather.4 = bf16[384,768]{1,0:T(8,128)(2,1)S(1)} all-gather(bf16[96,768]{1,0:T(8,128)(2,1)S(1)} %fusion.109), channel_id=6, replica_groups=mesh['seq'=4,'dp'=8] {'seq'}, dimensions={0}, use_global_device_ids=true | all-gather | bytes 737280 | tf_op jit(solution)/shard_map/all_gather | solution.py:140
  290.4 7.7 %all-gather.3 = bf16[384,768]{1,0:T(8,128)(2,1)S(1)} all-gather(bf16[96,768]{1,0:T(8,128)(2,1)S(1)} %fusion.110), channel_id=5, replica_groups=mesh['seq'=4,'dp'=8] {'seq'}, dimensions={0}, use_global_device_ids=true | all-gather | bytes 737280 | tf_op jit(solution)/shard_map/all_gather | solution.py:140
  306.8 38.8 %psum.7 = f32[6,768]{1,0:T(8,128)S(1)} all-reduce(f32[6,768]{1,0:T(8,128)S(1)} %stack.15), channel_id=1, replica_groups=mesh['seq'=4,'dp'=8] {'seq','dp'}, use_global_device_ids=true, to_apply=%region_28.29 | all-reduce | flops 4608 | bytes 36864 | tf_op jit(solution)/shard_map/psum | solution.py:243
  (344 shorter events, 118.3 us)
Async XLA Ops:
  7.2 60.5 %copy-start = (bf16[768,768]{1,0:T(8,128)(2,1)S(1)}, bf16[768,768]{1,0:T(8,128)(2,1)}, u32[]{:S(2)}) copy-start(bf16[768,768]{1,0:T(8,128)(2,1)} %param.33) | copy-start | bytes 3538948
  7.2 60.5 %all-gather.9.cloned.1.call-start = ((), (), s32[]{:S(2)}) async-start(), calls=%async_computation.8 | async-start | bytes 1966080 | tf_op jit(solution)/shard_map/all_gather | solution.py:140
  7.9 159.6 %reduce-scatter.7.cloned.1.call-start = ((), (), s32[]{:S(2)}) async-start(), calls=%async_computation.5 | async-start | bytes 983040 | tf_op jit(solution)/shard_map/reduce_scatter | solution.py:141
  10.7 13.0 %copy-start.53 = (f32[768]{0:T(1024)}, f32[768]{0:T(1024)S(1)}, u32[]{:S(2)}) copy-start(f32[768]{0:T(1024)S(1)} %convert_element_type.403) | copy-start | bytes 9220
  25.6 15.9 %copy-start.39 = (bf16[512,192]{0,1:T(8,128)(2,1)}, bf16[512,192]{0,1:T(8,128)(2,1)S(1)}, u32[]{:S(2)}) copy-start(bf16[512,192]{0,1:T(8,128)(2,1)S(1)} %convolution_convert_fusion.3) | copy-start | bytes 589828
  27.4 14.1 %copy-start.37 = (bf16[512,192]{0,1:T(8,128)(2,1)}, bf16[512,192]{0,1:T(8,128)(2,1)S(1)}, u32[]{:S(2)}) copy-start(bf16[512,192]{0,1:T(8,128)(2,1)S(1)} %convolution_convert_fusion.4) | copy-start | bytes 589828
  29.1 13.6 %copy-start.47 = (bf16[512,192]{0,1:T(8,128)(2,1)}, bf16[512,192]{0,1:T(8,128)(2,1)S(1)}, u32[]{:S(2)}) copy-start(bf16[512,192]{0,1:T(8,128)(2,1)S(1)} %convolution_convert_fusion.5) | copy-start | bytes 589828
  44.7 43.5 %copy-start.57 = (f32[768]{0:T(1024)}, f32[768]{0:T(1024)S(1)}, u32[]{:S(2)}) copy-start(f32[768]{0:T(1024)S(1)} %convert_element_type.425) | copy-start | bytes 9220
  67.7 27.1 %copy-start.19 = (bf16[1,512,768]{2,1,0:T(8,128)(2,1)}, bf16[1,512,768]{2,1,0:T(8,128)(2,1)S(1)}, u32[]{:S(2)}) copy-start(bf16[1,512,768]{2,1,0:T(8,128)(2,1)S(1)} %all-gather.2) | copy-start | bytes 2359300
  98.6 142.2 %reduce-scatter.5.cloned.1.call-start = ((), (), s32[]{:S(2)}) async-start(), calls=%async_computation.4 | async-start | bytes 983040 | tf_op jit(solution)/shard_map/reduce_scatter | solution.py:141
  102.6 15.9 %collective-permute-start.6 = (bf16[2,2,96,768]{3,2,1,0:T(8,128)(2,1)}, bf16[2,2,96,768]{3,2,1,0:T(8,128)(2,1)}, u32[]{:S(2)}, u32[]{:S(2)}) collective-permute-start(bf16[2,2,96,768]{3,2,1,0:T(8,128)(2,1)} %fusion.78), channel_id=1, source_target_pairs={{0,2},{1,3},{2,0},{3,1},{4,6},{5,7},{6,4},{7,5},{8,10},{9,11},{10,... | collective-permute-start | bytes 1769480 | tf_op jit(solution)/shard_map/ppermute | solution.py:72
  105.9 16.9 %collective-permute-start.9 = (bf16[2,2,96,768]{3,2,0,1:T(8,128)(2,1)}, bf16[2,2,96,768]{3,2,0,1:T(8,128)(2,1)}, u32[]{:S(2)}, u32[]{:S(2)}) collective-permute-start(bf16[2,2,96,768]{3,2,0,1:T(8,128)(2,1)} %fusion.79), channel_id=1, source_target_pairs={{0,1},{1,0},{2,3},{3,2},{4,5},{5,4},{6,7},{7,6},{8,9},{9,8},{10,11... | collective-permute-start | bytes 1769480 | tf_op jit(solution)/shard_map/ppermute | solution.py:72
  109.1 195.8 %reduce-scatter.9.cloned.1.call-start = ((), (), s32[]{:S(2)}) async-start(), calls=%async_computation.6 | async-start | bytes 983040 | tf_op jit(solution)/shard_map/reduce_scatter | solution.py:141
  120.2 15.8 %collective-permute-start.7 = (bf16[2,96,768]{2,1,0:T(8,128)(2,1)S(1)}, bf16[2,96,768]{2,1,0:T(8,128)(2,1)S(1)}, u32[]{:S(2)}, u32[]{:S(2)}) collective-permute-start(bf16[2,96,768]{2,1,0:T(8,128)(2,1)S(1)} %fusion.105), channel_id=1, source_target_pairs={{0,4},{1,5},{2,6},{3,7},{4,0},{5,1},{6,2},{7,3},{8,12},{9,13},{10,... | collective-permute-start | bytes 884744 | tf_op jit(solution)/shard_map/ppermute | solution.py:72
  124.0 13.6 %collective-permute-start.10 = (bf16[2,96,768]{2,1,0:T(8,128)(2,1)S(1)}, bf16[2,96,768]{2,1,0:T(8,128)(2,1)S(1)}, u32[]{:S(2)}, u32[]{:S(2)}) collective-permute-start(bf16[2,96,768]{2,1,0:T(8,128)(2,1)S(1)} %fusion.106), channel_id=1, source_target_pairs={{0,2},{1,3},{2,0},{3,1},{4,6},{5,7},{6,4},{7,5},{8,10},{9,11},{10,... | collective-permute-start | bytes 884744 | tf_op jit(solution)/shard_map/ppermute | solution.py:72
  136.1 5.2 %collective-permute-start.8 = (bf16[96,768]{1,0:T(8,128)(2,1)S(1)}, bf16[96,768]{1,0:T(8,128)(2,1)S(1)}, u32[]{:S(2)}, u32[]{:S(2)}) collective-permute-start(bf16[96,768]{1,0:T(8,128)(2,1)S(1)} %fusion.119), channel_id=1, source_target_pairs={{0,1},{1,0},{2,3},{3,2},{4,5},{5,4},{6,7},{7,6},{8,9},{9,8},{10,11... | collective-permute-start | bytes 442376 | tf_op jit(solution)/shard_map/ppermute | solution.py:72
  137.8 14.3 %collective-permute-start.11 = (bf16[96,768]{1,0:T(8,128)(2,1)S(1)}, bf16[96,768]{1,0:T(8,128)(2,1)S(1)}, u32[]{:S(2)}, u32[]{:S(2)}) collective-permute-start(bf16[96,768]{1,0:T(8,128)(2,1)S(1)} %fusion.120), channel_id=1, source_target_pairs={{0,4},{1,5},{2,6},{3,7},{4,0},{5,1},{6,2},{7,3},{8,12},{9,13},{10,... | collective-permute-start | bytes 442376 | tf_op jit(solution)/shard_map/ppermute | solution.py:72
  163.8 12.8 %copy-start.59 = (f32[768]{0:T(1024)S(1)}, f32[768]{0:T(1024)}, u32[]{:S(2)}) copy-start(f32[768]{0:T(1024)} %copy-done.57) | copy-start | bytes 9220
  163.8 12.8 %copy-start.62 = (f32[512]{0:T(512)S(1)}, f32[512]{0:T(512)}, u32[]{:S(2)}) copy-start(f32[512]{0:T(512)} %copy-done.60) | copy-start | bytes 6148
  163.8 12.8 %copy-start.71 = (f32[512]{0:T(512)S(1)}, f32[512]{0:T(512)}, u32[]{:S(2)}) copy-start(f32[512]{0:T(512)} %copy-done.69) | copy-start | bytes 6148
  163.8 18.7 %slice-start = ((s8[6291456]{0:T(1024)(128)(4,1)}), s8[2097152]{0:T(1024)(128)(4,1)S(1)}, s32[]{:S(2)}) async-start(s8[6291456]{0:T(1024)(128)(4,1)} %bitcast.262), calls=%async_computation.9 | async-start | bytes 4194304
  167.6 11.9 %copy-start.7 = (f32[512,768]{1,0:T(8,128)S(1)}, f32[512,768]{1,0:T(8,128)}, u32[]{:S(2)}) copy-start(f32[512,768]{1,0:T(8,128)} %copy-done.6) | copy-start | bytes 4718596
  167.6 11.9 %copy-start.21 = (bf16[1,512,768]{2,1,0:T(8,128)(2,1)S(1)}, bf16[1,512,768]{2,1,0:T(8,128)(2,1)}, u32[]{:S(2)}) copy-start(bf16[1,512,768]{2,1,0:T(8,128)(2,1)} %copy-done.19) | copy-start | bytes 2359300
  183.7 24.9 %copy-start.26 = (bf16[3,64,1024]{2,1,0:T(8,128)(2,1)}, bf16[3,64,1024]{2,1,0:T(8,128)(2,1)S(1)}, u32[]{:S(2)}) copy-start(bf16[3,64,1024]{2,1,0:T(8,128)(2,1)S(1)} %fusion.59) | copy-start | bytes 1179652
  188.8 20.3 %copy-start.24 = (bf16[3,64,1024]{2,1,0:T(8,128)(2,1)}, bf16[3,64,1024]{2,1,0:T(8,128)(2,1)S(1)}, u32[]{:S(2)}) copy-start(bf16[3,64,1024]{2,1,0:T(8,128)(2,1)S(1)} %fusion.52) | copy-start | bytes 1179652
  214.0 28.7 %collective-permute-start.3 = (bf16[2,2,96,768]{3,2,1,0:T(8,128)(2,1)}, bf16[2,2,96,768]{3,2,1,0:T(8,128)(2,1)}, u32[]{:S(2)}, u32[]{:S(2)}) collective-permute-start(bf16[2,2,96,768]{3,2,1,0:T(8,128)(2,1)} %fusion.77), channel_id=1, source_target_pairs={{0,1},{1,0},{2,3},{3,2},{4,5},{5,4},{6,7},{7,6},{8,9},{9,8},{10,11... | collective-permute-start | bytes 1769480 | tf_op jit(solution)/shard_map/ppermute | solution.py:72
  228.3 119.9 %reduce-scatter.11.cloned.1.call-start = ((), (), s32[]{:S(2)}) async-start(), calls=%async_computation.7 | async-start | bytes 1966080 | tf_op jit(solution)/shard_map/reduce_scatter | solution.py:141
  234.6 16.5 %collective-permute-start = (bf16[2,2,96,768]{3,2,1,0:T(8,128)(2,1)}, bf16[2,2,96,768]{3,2,1,0:T(8,128)(2,1)}, u32[]{:S(2)}, u32[]{:S(2)}) collective-permute-start(bf16[2,2,96,768]{3,2,1,0:T(8,128)(2,1)} %fusion.76), channel_id=1, source_target_pairs={{0,2},{1,3},{2,0},{3,1},{4,6},{5,7},{6,4},{7,5},{8,10},{9,11},{10,... | collective-permute-start | bytes 1769480 | tf_op jit(solution)/shard_map/ppermute | solution.py:72
  244.2 16.1 %collective-permute-start.4 = (bf16[2,96,768]{2,1,0:T(8,128)(2,1)S(1)}, bf16[2,96,768]{2,1,0:T(8,128)(2,1)S(1)}, u32[]{:S(2)}, u32[]{:S(2)}) collective-permute-start(bf16[2,96,768]{2,1,0:T(8,128)(2,1)S(1)} %fusion.104), channel_id=1, source_target_pairs={{0,2},{1,3},{2,0},{3,1},{4,6},{5,7},{6,4},{7,5},{8,10},{9,11},{10,... | collective-permute-start | bytes 884744 | tf_op jit(solution)/shard_map/ppermute | solution.py:72
  252.4 19.5 %collective-permute-start.1 = (bf16[2,96,768]{2,1,0:T(8,128)(2,1)S(1)}, bf16[2,96,768]{2,1,0:T(8,128)(2,1)S(1)}, u32[]{:S(2)}, u32[]{:S(2)}) collective-permute-start(bf16[2,96,768]{2,1,0:T(8,128)(2,1)S(1)} %fusion.103), channel_id=1, source_target_pairs={{0,4},{1,5},{2,6},{3,7},{4,0},{5,1},{6,2},{7,3},{8,12},{9,13},{10,... | collective-permute-start | bytes 884744 | tf_op jit(solution)/shard_map/ppermute | solution.py:72
  260.5 13.0 %collective-permute-start.5 = (bf16[96,768]{1,0:T(8,128)(2,1)S(1)}, bf16[96,768]{1,0:T(8,128)(2,1)S(1)}, u32[]{:S(2)}, u32[]{:S(2)}) collective-permute-start(bf16[96,768]{1,0:T(8,128)(2,1)S(1)} %fusion.118), channel_id=1, source_target_pairs={{0,4},{1,5},{2,6},{3,7},{4,0},{5,1},{6,2},{7,3},{8,12},{9,13},{10,... | collective-permute-start | bytes 442376 | tf_op jit(solution)/shard_map/ppermute | solution.py:72
  272.0 17.5 %collective-permute-start.2 = (bf16[96,768]{1,0:T(8,128)(2,1)S(1)}, bf16[96,768]{1,0:T(8,128)(2,1)}, u32[]{:S(2)}, u32[]{:S(2)}) collective-permute-start(bf16[96,768]{1,0:T(8,128)(2,1)S(1)} %fusion.117), channel_id=1, source_target_pairs={{0,1},{1,0},{2,3},{3,2},{4,5},{5,4},{6,7},{7,6},{8,9},{9,8},{10,11... | collective-permute-start | bytes 442376 | tf_op jit(solution)/shard_map/ppermute | solution.py:72
  (73 other events, 278.8 us)
Sparse Core Ops, SparseCore 0:
  9.6 22.3 all-gather.8
  98.7 23.8 reduce-scatter.6
  125.8 26.4 reduce-scatter.4
  228.5 22.4 reduce-scatter.8
  253.5 31.3 reduce-scatter.10

commit v2 on v1

v2 whole, which is shorter than its diff:
```python
import functools

import jax
import jax.numpy as jnp
from jax import lax
from jax.experimental import pallas as pl
from jax.experimental.pallas import tpu as pltpu
from jax.sharding import PartitionSpec as P

HEAD_DIM = 64
EPSILON = 1e-05
NEGATIVE = -1e30
F32 = jnp.float32
BF16 = jnp.bfloat16
MESH = pl.DeviceIdType.MESH
WINDOW = 256
CHUNKS = 2


def mm(left, right):
    return jnp.dot(left, right, preferred_element_type=F32)


def mm_t(left, right):
    return lax.dot_general(left, right, (((1,), (1,)), ((), ())), preferred_element_type=F32)


def t_mm(left, right):
    return lax.dot_general(left, right, (((0,), (0,)), ((), ())), preferred_element_type=F32)


def normalize(values):
    centered = values - jnp.mean(values, axis=-1, keepdims=True)
    rate = lax.rsqrt(jnp.mean(centered * centered, axis=-1, keepdims=True) + EPSILON)
    return centered * rate, rate


def norm_back(grad, gain, normed, rate):
    scaled = grad * gain
    inner = jnp.mean(scaled * normed, axis=-1, keepdims=True)
    return rate * (scaled - jnp.mean(scaled, axis=-1, keepdims=True) - normed * inner)


class Names:
    def __init__(self, names, refs):
        self.__dict__.update(zip(names, refs))


INPUTS = ["tokens", "memory", "out_grad", "target_ids", "memory_ids", "pads"]
INPUTS += ["w_sq", "w_sk", "w_sv", "w_so", "w_cq", "w_ck", "w_cv", "w_co", "w_fi", "w_fo"]
INPUTS += ["gain_a", "shift_a", "gain_c", "shift_c", "gain_f", "shift_f"]
OUTPUTS = ["o_layer", "o_tokens", "o_memory", "o_stats"]
GROUPS = ["g_fo", "g_fi", "g_cross", "g_self"]
ORDERS = ((1, 2, 0), (0, 1, 2))


def row_kernel(scratch_names, seq, direct, *refs):
    r = Names(INPUTS + OUTPUTS + (["o_sums"] if direct else GROUPS) + scratch_names, refs)
    me = lax.axis_index("seq")
    core = lax.rem(me, 2)
    chip = me // 2
    peer_c = me + 1 - 2 * core
    peer_x = lax.rem(me + 2, 4)
    span = r.tokens.shape[0]
    full, width = r.row.shape
    src_span = r.memory.shape[0]
    src_full = src_span * seq
    part = width // seq
    count = part // HEAD_DIM
    size = full // CHUNKS
    odd = core
    window = pl.ds(pl.multiple_of((me * part) // 128 * 128, 128), WINDOW)
    own_rows = pl.ds(pl.multiple_of(me * part, 64), part)
    own_span = pl.ds(pl.multiple_of(me * span, span), span)

    def pick(value):
        return jnp.where(odd == 1, value[:, 64 : 64 + part], value[:, :part])

    def place(value):
        empty = jnp.zeros((value.shape[0], WINDOW - part), value.dtype)
        return jnp.where(
            odd == 1,
            jnp.concatenate([empty, value], 1),
            jnp.concatenate([value, empty], 1),
        )

    loads = []

    def load(src, dst):
        copy = pltpu.make_async_copy(src, dst, r.load_sem.at[len(loads)])
        copy.start()
        loads.append(copy)
        return copy

    get_sq = load(r.w_sq.at[:, window], r.win_sq)
    get_sk = load(r.w_sk.at[:, window], r.win_sk)
    get_sv = load(r.w_sv.at[:, window], r.win_sv)
    get_tok = load(r.tokens, r.row.at[own_span])
    get_ck = load(r.w_ck.at[:, window], r.win_ck)
    get_cv = load(r.w_cv.at[:, window], r.win_cv)
    get_mem = load(r.memory, r.mem.at[pl.ds(pl.multiple_of(me * src_span, src_span), src_span)])
    get_so = load(r.w_so, r.all_so)
    get_cq = load(r.w_cq, r.all_cq)
    get_co = load(r.w_co, r.all_co)
    get_og = load(r.out_grad, r.grad_out.at[own_span])
    if direct:
        place_dp = lax.axis_index("dp")
        blocks, share = r.g_fo.shape[0] * 4, r.g_fo.shape[3]
        unit = share
        get_fi, get_fo = [], []
        for b in range(blocks):
            start = pl.multiple_of(b * (seq * unit) + chip * 128, 128)
            get_fi.append(load(r.w_fi.at[:, pl.ds(start, WINDOW)], r.wide_fi.at[b]))
            start = pl.multiple_of((b * seq + me) * unit, 16)
            get_fo.append(load(r.w_fo.at[pl.ds(start, unit)], r.own_fo.at[pl.ds(b * unit, unit)]))
    else:
        get_fi = [load(r.w_fi, r.own_fi)]
        get_fo = [load(r.w_fo, r.own_fo)]

    barrier = pltpu.get_barrier_semaphore()
    peers = [{"seq": peer_c}, {"seq": peer_x}]
    bits, peers_dp = [], []
    if direct:
        for level in range(3):
            bit = lax.rem(place_dp // 2**level, 2)
            bits.append(bit)
            peers_dp.append({"dp": place_dp + 2**level * (1 - 2 * bit)})
    for peer in peers + peers_dp:
        pl.semaphore_signal(barrier, inc=1, device_id=peer, device_id_type=MESH)
    pl.semaphore_wait(barrier, len(peers + peers_dp))
    peer_c_id, peer_x_id = peers

    sent, busy = [], []

    def send(src, dst, peer):
        at = len(sent)
        copy = pltpu.make_async_remote_copy(
            src_ref=src,
            dst_ref=dst,
            send_sem=r.send_sem.at[at],
            recv_sem=r.recv_sem.at[at],
            device_id=peer,
            device_id_type=MESH,
        )
        copy.start()
        sent.append(copy)
        busy.append(copy)
        return copy

    def finish(copies):
        for copy in copies:
            copy.wait_send()
            busy[:] = [other for other in busy if other is not copy]

    class Gather:
        def __init__(self, src, spot):
            self.spot = spot
            self.x = send(src, spot(me), peer_x_id)
            self.c = send(src, spot(me), peer_c_id)

        def relay(self):
            self.x.wait_recv()
            self.second = send(self.spot(peer_x), self.spot(peer_x), peer_c_id)

        def wait(self):
            self.c.wait_recv()
            self.second.wait_recv()

    def rows_at(ref, length):
        return lambda who: ref.at[pl.ds(pl.multiple_of(who * length, length), length)]

    tok = Gather(r.tokens, rows_at(r.row, span))
    mem = Gather(r.memory, rows_at(r.mem, src_span))

    def column(ids):
        return jnp.broadcast_to(ids.astype(F32), (128, ids.shape[1])).T[:, :1]

    target_ids = r.target_ids[...]
    memory_ids = r.memory_ids[...]
    self_code = jnp.where(
        lax.broadcasted_iota(jnp.int32, (1, full), 1) < full - r.pads[0, 0], target_ids, -1
    ).astype(F32)
    cross_code = jnp.where(
        lax.broadcasted_iota(jnp.int32, (1, src_full), 1) < src_full - r.pads[0, 1], memory_ids, -1
    ).astype(F32)
    target_col = column(target_ids)
    i_pos = lax.broadcasted_iota(jnp.int32, (full, full), 0)
    j_pos = lax.broadcasted_iota(jnp.int32, (full, full), 1)
    self_mask = ((target_col == self_code) & (j_pos <= i_pos)) | (i_pos == j_pos)
    r.self_bias[...] = jnp.where(self_mask, 0.0, NEGATIVE)
    r.target_col[...] = target_col
    r.cross_code[...] = cross_code

    def self_masked(scores, rows, reach):
        return scores + r.self_bias[rows, :reach]

    def cross_masked(scores, rows, reach):
        return jnp.where(r.target_col[rows, :] == r.cross_code[:, :reach], scores, NEGATIVE)

    gain_a, shift_a, gain_c, shift_c, gain_f, shift_f = (
        getattr(r, name)[...].astype(F32).reshape(1, width) for name in INPUTS[-6:]
    )
    if direct:
        from_row = lax.broadcasted_iota(jnp.int32, (WINDOW, WINDOW), 0)
        to_col = lax.broadcasted_iota(jnp.int32, (WINDOW, WINDOW), 1)
        skip = me * unit - chip * 128
        for copy in get_fi:
            copy.wait()
        for t in range(0, blocks * unit, WINDOW):
            total = None
            for b in range(t // unit, min(blocks, (t + WINDOW - 1) // unit + 1)):
                at = to_col + (t - b * unit)
                chosen = (from_row == at + skip) & (at >= 0) & (at < unit)
                term = mm(r.wide_fi[b], jnp.where(chosen, 1.0, 0.0).astype(BF16))
                total = term if total is None else total + term
            r.own_fi[:, t : t + WINDOW] = total.astype(BF16)

    get_tok.wait()
    tok.relay()
    for copy in (get_sq, get_sk, get_sv):
        copy.wait()
    tok.wait()
    row = r.row[...].astype(F32)
    normed, _ = normalize(row)
    r.n_attend[...] = normed.astype(BF16)
    h_attend = (normed * gain_a + shift_a).astype(BF16)
    r.h_attend[...] = h_attend
    r.after[...] = row

    def to_heads(value, ref, rows):
        for h in range(count):
            ref[h, rows, :] = value[:, h * HEAD_DIM : (h + 1) * HEAD_DIM].astype(ref.dtype)

    everything = slice(0, full)
    to_heads(pick(mm(h_attend, r.win_sq[...])) * HEAD_DIM**-0.5, r.q, everything)
    to_heads(pick(mm(h_attend, r.win_sk[...])), r.k, everything)
    to_heads(pick(mm(h_attend, r.win_sv[...])), r.v, everything)

    def attend(q, k, v, masked, weights, mixed, rows, reach):
        def one(h, carry):
            scores = masked(mm_t(q[h, rows, :], k[h, :reach, :]), rows, reach)
            highest = jnp.max(scores, axis=-1, keepdims=True)
            exponent = jnp.exp(scores - highest)
            total = jnp.sum(exponent, axis=-1, keepdims=True)
            low = exponent.astype(BF16)
            weights[h, rows, :reach] = low
            over = 1.0 / total
            mixed[h, rows, HEAD_DIM : HEAD_DIM + 1] = over
            mixed[h, rows, :HEAD_DIM] = mm(low, v[h, :reach, :]) * over
            return carry

        lax.fori_loop(0, count, one, 0)
        return jnp.concatenate([mixed[h, rows, :HEAD_DIM] for h in range(count)], axis=1).astype(BF16)

    def attend_back(q, k, v, grad, weights, mixed, grad_q, dk, dv, rows, reach, first):
        def one(h, carry):
            scaled = grad[h, rows, :].astype(F32) * mixed[h, rows, HEAD_DIM : HEAD_DIM + 1]
            inner = jnp.sum(scaled * mixed[h, rows, :HEAD_DIM], axis=-1, keepdims=True)
            low = scaled.astype(BF16)
            exponent = weights[h, rows, :reach]
            grad_weights = mm_t(low, v[h, :reach, :])
            grad_scores = (exponent.astype(F32) * (grad_weights - inner)).astype(BF16)
            grad_q[h, rows, :] = mm(grad_scores, k[h, :reach, :]) * HEAD_DIM**-0.5
            more_k = mm(q[h, rows, :].T, grad_scores)
            more_v = mm(low.T, exponent)
            if first:
                dk[h, :, :reach] = more_k
                dv[h, :, :reach] = more_v
            else:
                dk[h, :, :reach] += more_k
                dv[h, :, :reach] += more_v
            return carry

        lax.fori_loop(0, count, one, 0)
        return jnp.concatenate([grad_q[h, rows, :] for h in range(count)], axis=1).astype(BF16)

    chunks = [slice(c * size, (c + 1) * size) for c in range(CHUNKS)]

    def gather_columns(buffer, value, rows):
        buffer[me, rows, :] = value
        return Gather(buffer.at[me, rows], lambda who: buffer.at[who, rows])

    def joined(buffer, rows):
        return jnp.concatenate([buffer[s, rows, :] for s in range(seq)], axis=1)

    to_self = []
    for c, rows in enumerate(chunks):
        mixed = attend(
            r.q, r.k, r.v, self_masked, r.self_weights, r.self_mix, rows, rows.stop
        )
        to_self.append(gather_columns(r.self_parts, mixed, rows))
    mem.relay()
    for copy in (get_ck, get_cv, get_mem):
        copy.wait()
    mem.wait()
    out = Gather(r.out_grad, rows_at(r.grad_out, span))
    source = r.mem[...]
    every = slice(0, src_full)
    to_heads(pick(mm(source, r.win_ck[...])), r.mk, every)
    to_heads(pick(mm(source, r.win_cv[...])), r.mv, every)

    for copy in (get_so, get_cq):
        copy.wait()
    to_cross = []
    for c, rows in enumerate(chunks):
        to_self[c].relay()
        to_self[c].wait()
        mixed = joined(r.self_parts, rows)
        r.self_mixed[rows, :] = mixed
        after = r.after[rows, :] + mm(mixed, r.all_so[...])
        r.after[rows, :] = after
        normed, rate = normalize(after)
        r.n_cross[rows, :] = normed.astype(BF16)
        r.r_cross[rows, :] = rate
        hidden = (normed * gain_c + shift_c).astype(BF16)
        r.h_cross[rows, :] = hidden
        to_heads(pick(mm(hidden, r.all_cq[:, window])) * HEAD_DIM**-0.5, r.cq, rows)
        mixed = attend(
            r.cq, r.mk, r.mv, cross_masked, r.cross_weights, r.cross_mix, rows, src_full
        )
        to_cross.append(gather_columns(r.cross_parts, mixed, rows))

    for copy in [get_co, get_og] + get_fo + ([] if direct else get_fi):
        copy.wait()
    out.relay()
    out.wait()
    half = size // 2
    stats = {}

    def add(name, value):
        value = jnp.sum(value, axis=0, keepdims=True)
        stats[name] = stats[name] + value if name in stats else value

    class Total:
        def __init__(self, c, value):
            self.c = c
            self.keep = pl.ds(pl.multiple_of(core * half, half), half)
            other = pl.ds(pl.multiple_of((1 - core) * half, half), half)
            r.sum_send[c] = value.astype(BF16)
            self.step = send(r.sum_send.at[c, other], r.sum_core.at[c], peer_c_id)

        def second(self):
            self.step.wait_recv()
            value = r.sum_send[self.c, self.keep, :].astype(F32) + r.sum_core[self.c].astype(F32)
            r.sum_mid[self.c] = value.astype(BF16)
            self.step = send(r.sum_mid.at[self.c], r.sum_chip.at[self.c], peer_x_id)

        def third(self):
            self.step.wait_recv()
            value = r.sum_mid[self.c].astype(F32) + r.sum_chip[self.c].astype(F32)
            r.sum_full[self.c, self.keep, :] = value.astype(BF16)
            self.step = send(
                r.sum_full.at[self.c, self.keep], r.sum_full.at[self.c, self.keep], peer_c_id
            )

        def wait(self):
            self.step.wait_recv()
            return r.sum_full[self.c].astype(F32)

    lanes = 2 * part

    class Reduce:
        def __init__(self, group, half_at):
            self.group = getattr(r, GROUPS[group])
            self.at = 2 * group + half_at
            self.cols = pl.ds(half_at * lanes, lanes)
            self.order = ORDERS[half_at]
            self.step = 0

        def index(self, last):
            spots = [slice(None)] * 3
            for bit in self.order[: self.step]:
                spots[2 - bit] = bits[bit]
            bit = self.order[self.step]
            spots[2 - bit] = last(bits[bit])
            return tuple(spots) + (slice(None), self.cols)

        def start(self):
            inbox = (r.in_half, r.in_quarter, r.in_eighth)[self.step].at[self.at]
            away = self.index(lambda bit: 1 - bit)
            self.copy = send(self.group.at[away], inbox, peers_dp[self.order[self.step]])
            self.inbox = inbox

        def next(self):
            self.copy.wait_recv()
            keep = self.index(lambda bit: bit)
            value = self.group[keep].astype(F32) + self.inbox[...].astype(F32)
            if self.step < 2:
                self.group[keep] = value.astype(BF16)
                self.step += 1
                self.start()
            else:
                r.done[self.at] = value.astype(BF16)
                self.local = load(r.done.at[self.at], r.o_sums.at[self.at, me])
                spot = lambda who: r.o_sums.at[self.at, who]
                self.gather = Gather(r.done.at[self.at], spot)

    class Group:
        def __init__(self, group):
            self.halves = [Reduce(group, at) for at in range(2)]
            for part_of in self.halves:
                part_of.start()

        def next(self):
            for part_of in self.halves:
                part_of.next()

        def relay(self):
            for part_of in self.halves:
                part_of.gather.relay()

        def wait(self):
            for part_of in self.halves:
                part_of.local.wait()
                part_of.gather.wait()

    class Nothing:
        next = relay = wait = lambda self: None

    def reduced(group):
        return Group(group) if direct else Nothing()

    def put(group, at, value):
        ref = getattr(r, GROUPS[group])
        value = value.astype(BF16)
        if direct:
            value = value.reshape(2, 2, 2, share, value.shape[-1])
            ref[:, :, :, :, at : at + value.shape[-1]] = value
        else:
            ref[:, at : at + value.shape[-1]] = value

    totals = []
    for c, rows in enumerate(chunks):
        to_cross[c].relay()
        to_cross[c].wait()
        mixed = joined(r.cross_parts, rows)
        r.cross_mixed[rows, :] = mixed
        after = r.after[rows, :] + mm(mixed, r.all_co[...])
        r.after[rows, :] = after
        normed, rate = normalize(after)
        r.n_feed[rows, :] = normed.astype(BF16)
        r.r_feed[rows, :] = rate
        hidden = (normed * gain_f + shift_f).astype(BF16)
        r.h_feed[rows, :] = hidden
        upward = mm(hidden, r.own_fi[...])
        if c > 0:
            totals[c - 1].second()
        bell = 0.5 + 0.5 * lax.erf(upward * 2.0**-0.5)
        r.active[rows, :] = (upward * bell).astype(BF16)
        slope = bell + upward * jnp.exp(-0.5 * upward * upward) * 0.3989422804014327
        grad_up = (mm_t(r.grad_out[rows, :], r.own_fo[...]) * slope).astype(BF16)
        r.grad_up[rows, :] = grad_up
        back = mm_t(grad_up, r.own_fi[...])
        add("gf", back * normed)
        add("sf", back)
        totals.append(Total(c, back))
    scatter_rows = []

    class Scatter:
        def __init__(self, mail, core_in, chip_in, value):
            self.mail, self.core_in, self.chip_in = mail, core_in, chip_in
            mail[...] = value.reshape(mail.shape).astype(BF16)
            for spot in range(2):
                send(mail.at[2 * spot + 1 - core], core_in.at[spot], peer_c_id)
            self.steps = sent[-2:]

        def second(self):
            for step in self.steps:
                step.wait_recv()
            away = 1 - chip
            value = self.mail[2 * away + core].astype(F32) + self.core_in[away].astype(F32)
            self.mail[2 * away + core] = value.astype(BF16)
            self.step = send(self.mail.at[2 * away + core], self.chip_in, peer_x_id)

        def wait(self):
            self.step.wait_recv()
            value = self.mail[me].astype(F32) + self.core_in[chip].astype(F32)
            return value + self.chip_in[...].astype(F32)

    layer = Scatter(r.layer_mail, r.layer_core, r.layer_chip, mm(r.active[...], r.own_fo[...]))
    totals[0].third()
    totals[1].second()
    put(0, 0, t_mm(r.active[...], r.grad_out[...]))
    sum_fo = reduced(0)
    put(1, 0, t_mm(r.h_feed[...], r.grad_up[...]))
    sum_fi = reduced(1)
    layer.second()

    to_rows = []
    for c, rows in enumerate(chunks):
        grad = totals[c].wait()
        normed = r.n_feed[rows, :].astype(F32)
        grad = r.grad_out[rows, :].astype(F32) + norm_back(grad, gain_f, normed, r.r_feed[rows, :])
        r.grad_row[rows, :] = grad
        low = grad.astype(BF16)
        r.grad_cross[rows, :] = low
        to_heads(mm_t(low, r.all_co[own_rows, :]).astype(BF16), r.grad_mix, rows)
        if c == 0:
            totals[1].third()
        grad_rows = attend_back(
            r.cq, r.mk, r.mv, r.grad_mix, r.cross_weights, r.cross_mix, r.grad_q,
            r.grad_mk, r.grad_mv, rows, src_full, c == 0,
        )
        to_rows.append(gather_columns(r.row_parts, grad_rows, rows))
        if c == 0:
            r.o_layer[...] = r.after[own_span, :] + layer.wait()
    sum_fo.next()
    mk_t = r.grad_mk[...].reshape(part, src_full)
    mv_t = r.grad_mv[...].reshape(part, src_full)
    mk_low, mv_low = mk_t.astype(BF16), mv_t.astype(BF16)
    terms = mm_t(place(mk_t.T.astype(BF16)), r.win_ck[...]) + mm_t(
        place(mv_t.T.astype(BF16)), r.win_cv[...]
    )
    memory_sum = Scatter(r.mem_mail, r.mem_core, r.mem_chip, terms)
    to_rows[0].relay()
    put(2, part, mm(mk_low, r.mem[...]).T)
    put(2, 2 * part, mm(mv_low, r.mem[...]).T)
    put(2, 0, pick(t_mm(r.cross_mixed[...], r.grad_cross[:, window])))
    put(2, 3 * part, t_mm(r.h_cross[...], r.row_parts[me]))
    sum_cross = reduced(2)
    sum_fi.next()
    memory_sum.second()

    for c, rows in enumerate(chunks):
        if c > 0:
            to_rows[c].relay()
        to_rows[c].wait()
        grad = mm_t(joined(r.row_parts, rows), r.all_cq[...])
        normed = r.n_cross[rows, :].astype(F32)
        add("gc", grad * normed)
        add("sc", grad)
        grad = r.grad_row[rows, :] + norm_back(grad, gain_c, normed, r.r_cross[rows, :])
        r.grad_row[rows, :] = grad
        low = grad.astype(BF16)
        r.grad_self[rows, :] = low
        to_heads(mm_t(low, r.all_so[own_rows, :]).astype(BF16), r.grad_mix, rows)
    sum_fo.next()
    for c, rows in reversed(list(enumerate(chunks))):
        r.grad_rows[rows, :] = attend_back(
            r.q, r.k, r.v, r.grad_mix, r.self_weights, r.self_mix, r.grad_q,
            r.grad_k, r.grad_v, rows, rows.stop, c == CHUNKS - 1,
        )
    sum_fo.next()
    sum_fi.next()
    sum_cross.next()
    k_t = r.grad_k[...].reshape(part, full)
    v_t = r.grad_v[...].reshape(part, full)
    grad_q = r.grad_rows[...]
    back = (
        mm_t(place(grad_q), r.win_sq[...])
        + mm_t(place(k_t.T.astype(BF16)), r.win_sk[...])
        + mm_t(place(v_t.T.astype(BF16)), r.win_sv[...])
    )
    add("ga", back * r.n_attend[...].astype(F32))
    add("sa", back)
    finish(layer.steps + [layer.step])
    tokens_sum = Scatter(r.layer_mail, r.layer_core, r.layer_chip, back)
    put(3, part, t_mm(r.h_attend[...], grad_q))
    put(3, 2 * part, mm(k_t.astype(BF16), r.h_attend[...]).T)
    put(3, 3 * part, mm(v_t.astype(BF16), r.h_attend[...]).T)
    put(3, 0, pick(t_mm(r.self_mixed[...], r.grad_self[:, window])))
    sum_self = reduced(3)
    shared = jnp.where(me == 0, 1.0, 0.0)
    stats = jnp.concatenate(
        [stats["ga"], stats["sa"], stats["gc"] * shared, stats["sc"] * shared, stats["gf"], stats["sf"]]
        + [jnp.zeros((2, width), F32)],
        axis=0,
    )

    class Stats:
        def __init__(self):
            self.value, self.step = stats, 0

        def start(self):
            r.stat_out[self.step] = self.value
            peer = (peers + peers_dp)[self.step]
            self.copy = send(r.stat_out.at[self.step], r.stat_in.at[self.step], peer)

        def next(self):
            self.copy.wait_recv()
            self.value = self.value + r.stat_in[self.step]
            self.step += 1
            if self.step < 5:
                self.start()

    if direct:
        norm_sum = Stats()
        norm_sum.start()
    tokens_sum.second()
    sum_fi.next()
    sum_fo.relay()
    sum_cross.next()
    if direct:
        norm_sum.next()
    r.o_memory[...] = memory_sum.wait()
    own_row = r.row[own_span, :].astype(F32)
    normed, rate = normalize(own_row)
    grad = tokens_sum.wait()
    r.o_tokens[...] = r.grad_row[own_span, :] + norm_back(grad, gain_a, normed, rate)
    sum_fi.relay()
    if direct:
        norm_sum.next()
    sum_cross.next()
    sum_self.next()
    if direct:
        norm_sum.next()
    sum_cross.relay()
    sum_self.next()
    if direct:
        norm_sum.next()
    sum_self.next()
    if direct:
        norm_sum.next()
        stats = norm_sum.value
    r.o_stats[...] = stats
    sum_self.relay()
    for group in (sum_fo, sum_fi, sum_cross, sum_self):
        group.wait()
    finish(list(busy))


def row_call(seq, span, src_span, width, part, units, direct, operands):
    full, src_full = span * seq, src_span * seq
    count, size = part // HEAD_DIM, full // CHUNKS
    half = size // 2
    shapes = dict(
        row=((full, width), BF16),
        mem=((src_full, width), BF16),
        grad_out=((full, width), BF16),
        win_sq=((width, WINDOW), BF16),
        win_sk=((width, WINDOW), BF16),
        win_sv=((width, WINDOW), BF16),
        win_ck=((width, WINDOW), BF16),
        win_cv=((width, WINDOW), BF16),
        all_so=((width, width), BF16),
        all_cq=((width, width), BF16),
        all_co=((width, width), BF16),
        own_fi=((width, units), BF16),
        own_fo=((units, width), BF16),
        self_bias=((full, full), F32),
        target_col=((full, 1), F32),
        cross_code=((1, src_full), F32),
        n_attend=((full, width), BF16),
        n_cross=((full, width), BF16),
        n_feed=((full, width), BF16),
        r_cross=((full, 1), F32),
        r_feed=((full, 1), F32),
        h_attend=((full, width), BF16),
        h_cross=((full, width), BF16),
        h_feed=((full, width), BF16),
        after=((full, width), F32),
        grad_row=((full, width), F32),
        q=((count, full, HEAD_DIM), BF16),
        k=((count, full, HEAD_DIM), BF16),
        v=((count, full, HEAD_DIM), BF16),
        cq=((count, full, HEAD_DIM), BF16),
        mk=((count, src_full, HEAD_DIM), BF16),
        mv=((count, src_full, HEAD_DIM), BF16),
        grad_mix=((count, full, HEAD_DIM), BF16),
        grad_q=((count, full, HEAD_DIM), F32),
        self_weights=((count, full, full), BF16),
        cross_weights=((count, full, src_full), BF16),
        self_mix=((count, full, 2 * HEAD_DIM), F32),
        cross_mix=((count, full, 2 * HEAD_DIM), F32),
        grad_k=((count, HEAD_DIM, full), F32),
        grad_v=((count, HEAD_DIM, full), F32),
        grad_mk=((count, HEAD_DIM, src_full), F32),
        grad_mv=((count, HEAD_DIM, src_full), F32),
        self_parts=((seq, full, part), BF16),
        cross_parts=((seq, full, part), BF16),
        row_parts=((seq, full, part), BF16),
        self_mixed=((full, width), BF16),
        cross_mixed=((full, width), BF16),
        active=((full, units), BF16),
        grad_up=((full, units), BF16),
        grad_cross=((full, width), BF16),
        grad_self=((full, width), BF16),
        grad_rows=((full, part), BF16),
        sum_send=((CHUNKS, size, width), BF16),
        sum_core=((CHUNKS, half, width), BF16),
        sum_mid=((CHUNKS, half, width), BF16),
        sum_chip=((CHUNKS, half, width), BF16),
        sum_full=((CHUNKS, size, width), BF16),
        layer_mail=((seq, span, width), BF16),
        layer_core=((2, span, width), BF16),
        layer_chip=((span, width), BF16),
        mem_mail=((seq, src_span, width), BF16),
        mem_core=((2, src_span, width), BF16),
        mem_chip=((src_span, width), BF16),
    )
    group = (width, 4 * part)
    if direct:
        blocks, share = 8, width // 8
        lanes = 2 * part
        group = (2, 2, 2, share, 4 * part)
        shapes.update({name: (group, BF16) for name in GROUPS})
        shapes.update(
            wide_fi=((blocks, width, WINDOW), BF16),
            in_half=((8, 2, 2, share, lanes), BF16),
            in_quarter=((8, 2, share, lanes), BF16),
            in_eighth=((8, share, lanes), BF16),
            done=((8, share, lanes), BF16),
            stat_out=((5, 8, width), F32),
            stat_in=((5, 8, width), F32),
        )
    names = list(shapes) + ["load_sem", "send_sem", "recv_sem"]
    scratch = [pltpu.VMEM(shape, dtype) for shape, dtype in shapes.values()]
    scratch += [pltpu.SemaphoreType.DMA((40,)), pltpu.SemaphoreType.DMA((104,)), pltpu.SemaphoreType.DMA((104,))]
    hbm = pl.BlockSpec(memory_space=pl.ANY)
    vmem = pl.BlockSpec(memory_space=pltpu.VMEM)
    smem = pl.BlockSpec(memory_space=pltpu.SMEM)
    outs = [((span, width), F32), ((span, width), F32), ((src_span, width), F32), ((8, width), F32)]
    out_specs = [vmem] * 4
    if direct:
        outs += [((8, seq, share, lanes), BF16)]
        out_specs += [hbm]
    else:
        outs += [(group, BF16)] * 4
        out_specs += [vmem] * 4
    return pl.pallas_call(
        functools.partial(row_kernel, names, seq, direct),
        out_shape=[jax.ShapeDtypeStruct(s, t) for s, t in outs],
        in_specs=[hbm] * 3 + [vmem] * 2 + [smem] + [hbm] * 10 + [vmem] * 6,
        out_specs=out_specs,
        scratch_shapes=scratch,
        compiler_params=pltpu.CompilerParams(
            collective_id=0, has_side_effects=True, vmem_limit_bytes=64 * 2**20 - 2**17
        ),
    )(*operands)


def final_kernel(seq, dp, layer, tokens, memory, stats, sums, *refs):
    outs, sems = refs[:-1], refs[-1]
    copies = [
        pltpu.make_async_copy(src, dst, sems.at[i])
        for i, (src, dst) in enumerate(zip((layer, tokens, memory), outs[:3]))
    ]
    for copy in copies:
        copy.start()
    sq, sk, sv, so, cq, ck, cv, co, fi, fo = outs[3:13]
    share, lanes = sums.shape[2:]
    part = lanes // 2
    unit = fo.shape[0] // seq
    for s in range(seq):
        for at in range(2):
            fo[s * unit : (s + 1) * unit, at * lanes : (at + 1) * lanes] = sums[at, s].astype(F32)
    for at in range(2):
        wide = [sums[2 + at, s].astype(F32) for s in range(seq)]
        for b in range(dp // 2):
            block = [w[:, b * unit : (b + 1) * unit] for w in wide]
            start = (at * (dp // 2) + b) * seq * unit
            fi[:, start : start + seq * unit] = jnp.concatenate(block, 1)
    for i, out in enumerate((co, ck, cv, cq, so, sq, sk, sv)):
        start = i % 2 * part
        block = [sums[4 + i // 2, s].astype(F32)[:, start : start + part] for s in range(seq)]
        out[...] = jnp.concatenate(block, 1)
    width = stats.shape[1]
    back = lax.rem(width - lax.axis_index("dp") * share, width)
    own = pltpu.roll(stats[...], back, 1)[:, :share]
    for i, out in enumerate(outs[13:]):
        out[...] = own[i]
    for copy in copies:
        copy.wait()


def final_call(seq, dp, layer, tokens, memory, stats, sums):
    share, width = sums.shape[2], stats.shape[1]
    feed = sums.shape[3] * 2 * seq
    hbm = pl.BlockSpec(memory_space=pl.ANY)
    vmem = pl.BlockSpec(memory_space=pltpu.VMEM)
    shapes = [layer.shape, tokens.shape, memory.shape] + [(share, width)] * 8
    shapes += [(share, feed), (feed // dp, width)] + [(share,)] * 6
    return pl.pallas_call(
        functools.partial(final_kernel, seq, dp),
        out_shape=[jax.ShapeDtypeStruct(shape, F32) for shape in shapes],
        in_specs=[hbm] * 3 + [vmem] * 2,
        out_specs=[hbm] * 3 + [vmem] * 16,
        scratch_shapes=[pltpu.SemaphoreType.DMA((3,))],
        compiler_params=pltpu.CompilerParams(vmem_limit_bytes=32 * 2**20),
    )(layer, tokens, memory, stats, sums)


def swap(value, axis, bit):
    size = lax.axis_size(axis)
    return lax.ppermute(value, axis, [(i, i ^ bit) for i in range(size)])


def scatter_sum(value, bits):
    index = lax.axis_index("dp")
    size = lax.axis_size("dp")
    levels = size.bit_length() - 1
    blocks = value.reshape((2,) * levels + value.shape[1:])
    left = list(range(levels))[::-1]
    for bit in bits:
        at = left.index(bit)
        mine = (index >> bit) & 1
        keep = lax.dynamic_index_in_dim(blocks, mine, at, keepdims=False)
        away = lax.dynamic_index_in_dim(blocks, 1 - mine, at, keepdims=False)
        left.pop(at)
        got = swap(away.astype(BF16), "dp", 1 << bit)
        blocks = keep.astype(F32) + got.astype(F32)
    return blocks


def shards(
    tokens,
    memory,
    target_segments,
    memory_segments,
    pad_counts,
    out_grad,
    self_query,
    self_key,
    self_value,
    self_out,
    cross_query,
    cross_key,
    cross_value,
    cross_out,
    feed_in,
    feed_out,
    gain_attend,
    shift_attend,
    gain_cross,
    shift_cross,
    gain_feed,
    shift_feed,
):
    seq, dp = lax.axis_size("seq"), lax.axis_size("dp")
    me = lax.axis_index("seq")
    span, width = tokens.shape[1:]
    part = width // seq
    feed = feed_in.shape[1]
    unit = feed // dp // seq
    direct = dp == 8 and unit == width // dp and unit % 16 == 0
    fi, fo = feed_in, feed_out
    if not direct:
        fi = lax.dynamic_index_in_dim(fi.reshape(width, dp, seq, unit), me, 2, keepdims=False)
        fi = fi.reshape(width, dp * unit)
        fo = lax.dynamic_index_in_dim(fo.reshape(dp, seq, unit, width), me, 1, keepdims=False)
        fo = fo.reshape(dp * unit, width)
    operands = (
        tokens[0], memory[0], out_grad[0], target_segments, memory_segments, pad_counts,
        self_query, self_key, self_value, self_out, cross_query, cross_key, cross_value, cross_out,
        fi, fo, gain_attend, shift_attend, gain_cross, shift_cross, gain_feed, shift_feed,
    )
    results = row_call(seq, span, memory.shape[1], width, part, dp * unit, direct, operands)
    if direct:
        results = final_call(seq, dp, *results)
        return tuple(value[None] for value in results[:3]) + tuple(results[3:])
    layer_out, tokens_grad, memory_grad, stats, g_fo, g_fi, g_cross, g_self = results
    gather = lambda v, axis: lax.all_gather(v, "seq", axis=axis, tiled=True)

    levels = dp.bit_length() - 1
    up = list(range(levels))
    first, second = up, up[1:] + up[:1]
    share = width // dp
    split = lambda v: v.reshape(dp, share, -1)
    groups = ((split(g_fo), first), (split(g_fi), second), (split(g_cross), first), (split(g_self), second))
    summed = [gather(scatter_sum(v, bits).astype(BF16)[None], 0) for v, bits in groups]
    whole_fo = summed[0].reshape(seq * share, width).astype(F32)
    whole_fi = (
        summed[1].reshape(seq, share, dp, unit).transpose(1, 2, 0, 3).reshape(share, feed)
    ).astype(F32)

    def whole(group, at):
        block = group[:, :, at * part : (at + 1) * part]
        return block.transpose(1, 0, 2).reshape(share, width).astype(F32)

    co, ck, cv, cq = (whole(summed[2], at) for at in range(4))
    so, sq, sk, sv = (whole(summed[3], at) for at in range(4))
    stats = lax.psum(stats, ("seq", "dp"))
    norm_part = lax.dynamic_slice_in_dim(stats, lax.axis_index("dp") * share, share, 1)
    return (
        layer_out[None],
        tokens_grad[None],
        memory_grad[None],
        sq,
        sk,
        sv,
        so,
        cq,
        ck,
        cv,
        co,
        whole_fi,
        whole_fo,
    ) + tuple(norm_part[i] for i in range(6))


def solution(mesh):
    rows = P("dp", "seq", None)
    in_specs = (rows, rows, P("dp", None), P("dp", None), P("dp", None), rows) + (P(),) * 16
    out_specs = (rows,) * 3 + (P("dp", None),) * 10 + (P("dp"),) * 6
    return jax.shard_map(shards, mesh=mesh, in_specs=in_specs, out_specs=out_specs, check_vma=False)
```

time: 364 us -> 131 us (0.36); the launches traced: 357 us -> 131 us
  blocking collectives: 131 us -> 0 us
  Pallas kernels: 0 us -> 124 us
  matrix products: 61.6 us -> 0 us
  waiting for transfers between devices: 46.6 us -> 0 us
  local copies, waits for them, and re-layouts: 50.9 us -> 5.52 us
  other arithmetic: 34 us -> 0 us
  starting transfers between devices: 16.5 us -> 0 us
  between operations: 17 us -> 0.89 us
    pallas_call x0 -> x2, Pallas kernels: none -> 124 us  [the longest x1 120 us: row_call(): pl.pallas_call(functools.partial(row_kernel, names, seq, direct), out_sha...]
    all_gather x10 -> x0, blocking collectives: 91.8 us -> none  [shards(): gather = lambda v, axis: lax.all_gather(v, 'seq', axis=axis, tiled=True)]
    dot_general x42 -> x0, matrix products: 61.6 us -> none  [the longest x10 20.4 us: mm(): return jnp.dot(left, right, preferred_element_type=F32)]
    ppermute x12 -> x0, waiting for transfers between devices: 45.8 us -> none  [swap(): return lax.ppermute(value, axis, [(i, i ^ bit) for i in range(size)])]
    psum x1 -> x0, blocking collectives: 38.8 us -> none  [shards(): stats = lax.psum(stats, ('seq', 'dp'))]
    convert_element_type x31 -> x0, local copies, waits for them, and re-layouts: 24.7 us -> none  [the longest x16 11.5 us: whole(): return block.transpose(1, 0, 2).reshape(share, width).astype(F32)]
    ppermute x12 -> x0, starting transfers between devices: 16.1 us -> none  [swap(): return lax.ppermute(value, axis, [(i, i ^ bit) for i in range(size)])]
    convert_element_type x18 -> x0, other arithmetic: 12.3 us -> none  [the longest x2 5.13 us: attend_back(): grad_scores = (weights * (grad_weights - inner)).astype(BF16)]
  transfers between devices with their start and end apart: 17 -> 0, of which waited for: 7 -> 0; matrix products, arithmetic and copies ran while one was open for 33% -> 0% of each run, Pallas kernels for 0% -> 0%
where the time goes in v2:
time: 131 us
  Pallas kernels  124 us (95%)
  local copies, waits for them, and re-layouts  5.52 us (4%)
    pallas_call x1, Pallas kernels, row_call(): pl.pallas_call(functools.partial(row_kernel, names, seq, direct), out_sha...  120 us
    unnamed x10, local copies, waits for them, and re-layouts  5.52 us
    pallas_call x1, Pallas kernels, final_call(): pl.pallas_call(functools.partial(final_kernel, seq, dp), out_shape=[jax.S...  3.84 us

profile of v2, /device:TPU:0, one launch (start us, length us, event | category | flops | bytes accessed | tf_op | source)
XLA Modules:
  0.0 130.7 jit_solution(14258991854258267102)
XLA Ops:
  0.7 120.5 %shard_map.357 = (f32[128,768]{1,0:T(8,128)}, f32[128,768]{1,0:T(8,128)}, f32[256,768]{1,0:T(8,128)}, f32[8,768]{1,0:T(8,128)}, bf16[8,4,96,384]{3,2,1,0:T(8,128)(2,1)}) custom-call(bf16[128,768]{1,0:T(8,128)(2,1)} %bitcast.7, bf16[256,768]{1,0:T(8,128)(2,1)} %bitcast.6, bf16[128,768]{1,0:T(8,128)(2,1)} %bitcast.8, s32[1,512]{1,0:T(1,128)} %refs_3_.1, ...), custom_call_target="tpu_custom_call" | custom-call | tf_op jit(solution)/shard_map/pallas_call | solution.py:720
  121.2 0.0 copy-start
  121.2 1.7 %copy-done = bf16[8,4,96,384]{3,2,1,0:T(8,128)(2,1)S(1)} copy-done((bf16[8,4,96,384]{3,2,1,0:T(8,128)(2,1)S(1)}, bf16[8,4,96,384]{3,2,1,0:T(8,128)(2,1)}, u32[]{:S(2)}) %copy-start) | copy-done | bytes 2359320
  122.8 0.0 copy-start.1
  122.8 1.1 copy-done.1
  124.0 0.0 copy-start.2
  124.0 1.0 copy-done.2
  125.0 0.0 copy-start.3
  125.0 1.0 copy-done.3
  126.0 0.0 copy-start.4
  126.0 0.7 copy-done.4
  126.7 3.8 %shard_map.358 = (f32[128,768]{1,0:T(8,128)}, f32[128,768]{1,0:T(8,128)}, f32[256,768]{1,0:T(8,128)}, f32[96,768]{1,0:T(8,128)}, f32[96,768]{1,0:T(8,128)}, /*in...) custom-call(f32[128,768]{1,0:T(8,128)S(1)} %copy-done.2, ...), custom_call_target="tpu_custom_call" | custom-call | tf_op jit(solution)/shard_map/pallas_call | solution.py:773
Async XLA Ops:
  121.2 1.7 %copy-start = (bf16[8,4,96,384]{3,2,1,0:T(8,128)(2,1)S(1)}, bf16[8,4,96,384]{3,2,1,0:T(8,128)(2,1)}, u32[]{:S(2)}) copy-start(bf16[8,4,96,384]{3,2,1,0:T(8,128)(2,1)} %get-tuple-element.47.sums) | copy-start | bytes 7077892
  122.8 1.1 copy-start.1
  124.0 1.0 copy-start.2
  125.0 1.0 copy-start.3
  126.0 0.7 copy-start.4
